TPU v7x, 256 devices: a whole 4x4x8 slice. The times are simulated.
256 devices in a mesh: tg: 4 (over x), tile: 64 (over z, y, core).
Axes of the slice: x: 4, y: 4, z: 8, core: 2. Of those that a mesh axis runs over, the one named last changes fastest.
Arguments:
- age_cell: int32 [4, 4194304], P('tg', 'tile'), may hold values from 0 to 127
- dur_cell: int32 [4, 4194304], P('tg', 'tile'), may hold values from 0 to 3
- trans_code: int32 [4, 4194304], P('tg', 'tile'), may hold values from 0 to 15
- age_frac: float32 [4, 4194304], P('tg', 'tile'), may hold values from 0 to 1
- dur_frac: float32 [4, 4194304], P('tg', 'tile'), may hold values from 0 to 1
- exposure: float32 [4, 4194304], P('tg', 'tile'), may hold values from 0.05 to 1
- claims: float32 [4, 4194304], P('tg', 'tile'), may hold values from 0.01 to 1
- block_tile: int32 [4, 32768, 1], P('tg', 'tile'), may hold values from 0 to 63; in each aligned block of 512 rows (0 to 511, 512 to 1023, ..., all dimensions but the last counted through in order) at most 16 rows name the same one
- smooth_age: float32 [64], P('tg'), may hold values from 0.5 to 8
- smooth_dur: float32 [64], P('tg'), may hold values from 0.5 to 8
- credibility: float32 [64], P('tg'), may hold values from 0.2 to 2
Outputs:
- smoothed: float32 [64, 256, 128], P('tg', 'tile')
- residual: float32 [64, 256, 128], P('tg', 'tile')
Inputs may be any that keep to these rules, and one draw needn't show every extreme that they name: `block_tile`: among the 512 blocks of one device, no tile is named by more than 16 blocks.
All inputs are finite; a program needn't handle non-finite values.
Results may differ from a plain program's by a relative error of at most 0.0074.
Values sent between devices are 32-bit elements; how exact they have to be, the bound alone decides.
A program may use at most 64 MiB of HBM per device.

v0:
```python
import jax
import jax.numpy as jnp
from jax import lax
from jax.sharding import Mesh
from jax.sharding import PartitionSpec as P

AGE = 128
DT = 4
ITERS = 4
TILE = ("tile_0", "tile_1", "tile_2")


def shifted(value, axis, by):
    peers = lax.axis_size(axis)
    pairs = [(i, i + by) for i in range(peers) if 0 <= i + by < peers]
    return lax.ppermute(value, axis, pairs)


def joined_along(parts, dim):
    parts = jnp.moveaxis(parts, 0, dim)
    lengths = parts.shape
    return parts.reshape(*lengths[:dim], lengths[dim] * lengths[dim + 1], *lengths[dim + 2 :])


def all_blocks(value, axes, sequence):
    parts = value[None]
    for k in sequence:
        parts = lax.all_gather(parts, axes[k], axis=0, tiled=True)
    block = [lax.axis_size(axes[k]) for k in reversed(sequence)]
    parts = parts.reshape(*block, *value.shape)
    turned = sorted(range(len(sequence)), key=lambda place: sequence[len(sequence) - 1 - place])
    return parts.transpose(*turned, *range(len(sequence), parts.ndim)).reshape(-1, *value.shape)


def whole_of(value, axes, sequence, dim):
    return joined_along(all_blocks(value, axes, sequence), dim)


def from_everyone(value, axis):
    copies = jnp.broadcast_to(value, (lax.axis_size(axis), *value.shape))
    return lax.all_to_all(copies, axis, split_axis=0, concat_axis=0, tiled=True)


def over_copies(value, axis):
    everything = from_everyone(value, axis)
    return jnp.sum(everything, axis=0)


def spline(frac):
    rest = 1.0 - frac
    cube = frac * frac * frac
    return (
        rest * rest * rest / 6.0,
        (3.0 * cube - 6.0 * frac * frac + 4.0) / 6.0,
        (-3.0 * cube + 3.0 * frac * frac + 3.0 * frac + 1.0) / 6.0,
        cube / 6.0,
    )


def penalty_matrix(padded_grid, axis, first, record_count):
    inner_product = padded_grid.shape[axis] - 2

    def part(array, lower, length):
        return lax.slice_in_dim(array, lower, lower + length, axis=axis)

    differenced_values = (
        part(padded_grid, 0, inner_product)
        - 2.0 * part(padded_grid, 1, inner_product)
        + part(padded_grid, 2, inner_product)
    )
    layout = [1] * padded_grid.ndim
    layout[axis] = inner_product
    place_indices = first - 2 + lax.iota(jnp.int32, inner_product).reshape(layout)
    differenced_values = jnp.where(
        (place_indices >= 0) & (place_indices <= record_count - 3), differenced_values, 0.0
    )
    final_result = inner_product - 2
    return (
        part(differenced_values, 2, final_result)
        - 2.0 * part(differenced_values, 1, final_result)
        + part(differenced_values, 0, final_result)
    )


def factors(fields, trans_dev):
    ages, offsets, codes, age_position, dur_pos, expo, claim = fields
    record_count = ages.shape[0]
    age_w = spline(age_position)
    dur_w = spline(dur_pos)
    columns = lax.iota(jnp.int32, AGE)
    window = lax.iota(jnp.int32, DT + 3)
    age_table = jnp.zeros((record_count, AGE), jnp.float32)
    dur_table = jnp.zeros((record_count, DT + 3), jnp.float32)
    for place in range(4):
        age_table = age_table + jnp.where(
            columns[None, :] == (ages + place - 1)[:, None], age_w[place][:, None], 0.0
        )
        dur_table = dur_table + jnp.where(
            window[None, :] == (offsets + place)[:, None], dur_w[place][:, None], 0.0
        )
    values = jnp.stack([expo, claim], axis=1)
    scaled = dur_table[:, :, None] * values[:, None, :]
    onehot = (lax.iota(jnp.int32, trans_dev)[None, :] == codes[:, None]).astype(jnp.float32)
    left = (scaled[:, :, :, None] * onehot[:, None, None, :]).astype(jnp.bfloat16)
    return (left.reshape(record_count, -1), age_table.astype(jnp.bfloat16))


def per_device(
    age_cell,
    dur_cell,
    trans_code,
    age_frac,
    dur_frac,
    exposure,
    claims,
    block_tile,
    smooth_age,
    smooth_dur,
    credibility,
):
    trans_dev = smooth_age.shape[0]
    tiles = lax.axis_size(TILE)
    dur_all = tiles * DT
    start = lax.axis_index(TILE) * DT
    tile_ids = block_tile.reshape(-1)
    blocks = tile_ids.shape[0]
    record_fields = (age_cell, dur_cell, trans_code, age_frac, dur_frac, exposure, claims)
    capacity = max(2, 2 * blocks // tiles)
    onehot = (tile_ids[:, None] == lax.iota(jnp.int32, tiles)[None, :]).astype(jnp.int32)
    before = jnp.cumsum(onehot, axis=0) - onehot
    slots = jnp.sum(before * onehot, axis=1)
    target = tile_ids * capacity + slots
    packed = jnp.stack([field.reshape(blocks, 128).astype(jnp.float32) for field in record_fields])
    outgoing = jnp.zeros((7, tiles * capacity, 128), jnp.float32).at[:, target].set(packed)
    arrived = lax.all_to_all(
        outgoing.reshape(7, tiles, capacity * 128), TILE, split_axis=1, concat_axis=1, tiled=True
    )
    arrived = arrived.reshape(7, 16, -1)

    def owner_step(accum, item):
        fields = (
            item[0].astype(jnp.int32),
            item[1].astype(jnp.int32),
            item[2].astype(jnp.int32),
            item[3],
            item[4],
            item[5],
            item[6],
        )
        left, age_table = factors(fields, trans_dev)
        return (
            accum + jnp.einsum("rk,ra->ka", left, age_table, preferred_element_type=jnp.float32),
            None,
        )

    initial = jnp.zeros(((DT + 3) * 2 * trans_dev, AGE), jnp.float32)
    accum, _ = lax.scan(owner_step, initial, tuple((arrived[index] for index in range(7))))
    window = accum.reshape(DT + 3, 2 * trans_dev, AGE)
    from_below = shifted(window[DT + 1 : DT + 3], TILE, 1)
    from_above = shifted(window[0:1], TILE, -1)
    owned = window[1 : DT + 1]
    owned = owned.at[0:2].add(from_below)
    owned = owned.at[DT - 1 : DT].add(from_above)
    owned = whole_of(owned, TILE, (1, 0, 2), 0)
    rows_here = owned.shape[0]
    split = owned.reshape(rows_here, 2, trans_dev, AGE)
    pooled = over_copies(jnp.sum(split, axis=2), "tg")
    prior = pooled[:, 1] / (1.0 + pooled[:, 0])
    expo_grid = jnp.transpose(split[:, 0], (1, 0, 2))
    claim_grid = jnp.transpose(split[:, 1], (1, 0, 2))
    weight_a = smooth_age[:, None, None]
    weight_d = smooth_dur[:, None, None]
    cred = credibility[:, None, None]
    diagonal = expo_grid + cred

    def squares(values):
        local = jnp.sum(values * values, axis=(1, 2))
        return local

    right_side = claim_grid + cred * prior[None]
    smoothed = jnp.zeros_like(right_side)
    residual = right_side
    direction = right_side
    norm_now = squares(residual)
    for turn in range(ITERS):
        along_age = penalty_matrix(jnp.pad(direction, ((0, 0), (0, 0), (2, 2))), 2, 0, AGE)
        along_dur = penalty_matrix(jnp.pad(direction, ((0, 0), (2, 2), (0, 0))), 1, 0, dur_all)
        image = diagonal * direction + weight_a * along_age + weight_d * along_dur
        curvature_local = jnp.sum(direction * image, axis=(1, 2))
        alpha = norm_now / curvature_local
        smoothed = smoothed + alpha[:, None, None] * direction
        residual = residual - alpha[:, None, None] * image
        norm_next = squares(residual)
        direction = residual + (norm_next / norm_now)[:, None, None] * direction
        norm_now = norm_next
    smoothed = lax.dynamic_slice_in_dim(smoothed, start, DT, 1)
    residual = lax.dynamic_slice_in_dim(residual, start, DT, 1)
    return (smoothed, residual)


def solution(mesh):
    split = Mesh(
        mesh.devices.reshape(mesh.shape["tg"], 8, 4, 2), ("tg", "tile_0", "tile_1", "tile_2")
    )
    placed = (
        P("tg", TILE),
        P("tg", TILE),
        P("tg", TILE),
        P("tg", TILE),
        P("tg", TILE),
        P("tg", TILE),
        P("tg", TILE),
        P("tg", TILE, None),
        P("tg"),
        P("tg"),
        P("tg"),
    )
    return jax.shard_map(
        per_device,
        mesh=split,
        in_specs=placed,
        out_specs=(P("tg", TILE, None), P("tg", TILE, None)),
        check_vma=False,
    )
```

profile of v0, /device:TPU:1, one launch (start us, length us, event | category | flops | bytes accessed | tf_op | source)
XLA Modules:
  0.0 721.4 jit_solution(3579777054723532906)
XLA Ops:
  20.5 47.4 %scatter_fusion = f32[7,1024,128]{2,0,1:T(8,128)} fusion(f32[7,1024,128]{2,0,1:T(8,128)} %broadcast_in_dim.221, s32[512]{0:T(512)S(1)} %bitcast.173, f32[512,7,128]{2,1,0:T(8,128)S(1)} %bitcast.154), kind=kCustom, calls=%fused_computation | custom fusion | bytes 5507072 | tf_op jit(solution)/shard_map/scatter | solution.py:134
  67.9 13.3 %all-to-all-start = ((f32[7,64,2048]{2,0,1:T(8,128)}), f32[7,64,2048]{2,0,1:T(8,128)}, u32[]{:S(2)}, u32[]{:S(2)}) async-start(f32[7,64,2048]{2,0,1:T(8,128)} %bitcast.153), calls=%async_computation | async-start | bytes 8388608 | tf_op jit(solution)/shard_map/all_to_all | solution.py:135
  81.5 94.2 %all-to-all-done = f32[7,64,2048]{2,0,1:T(8,128)} async-done(((f32[7,64,2048]{2,0,1:T(8,128)}), f32[7,64,2048]{2,0,1:T(8,128)}, u32[]{:S(2)}, u32[]{:S(2)}) %all-to-all-start) | async-done | bytes 3670048 | tf_op jit(solution)/shard_map/all_to_all | solution.py:135
  175.7 22.5 %slice_reduce_fusion = (f32[64,2048]{1,0:T(8,128)S(1)}, f32[64,2048]{1,0:T(8,128)S(1)}, f32[64,2048]{1,0:T(8,128)S(1)}, f32[64,2048]{1,0:T(8,128)S(1)}, f32[64,2...) fusion(f32[7,64,2048]{2,0,1:T(8,128)} %all-to-all-done), kind=kLoop, calls=%fused_computation.158 | loop fusion | bytes 7340032 | tf_op jit(solution)/shard_map/slice | solution.py:157
  202.5 374.4 %while.18 = (s32[]{:T(128)}, f32[224,128]{1,0:T(8,128)S(1)}, f32[16,8192]{1,0:T(8,128)}, f32[16,8192]{1,0:T(8,128)}, f32[16,8192]{1,0:T(8,128)S(1)}, /*index=5*/...) while((s32[]{:T(128)}, f32[224,128]{1,0:T(8,128)S(1)}, ...), condition=%wide.region_5.6_spmd.clone, body=%wide.region_4.5_spmd.clone.sunk | while | flops 487497728 | bytes 11796615 | solution.py:157
  207.6 18.3 %fusion.102 = f32[224,128]{1,0:T(8,128)S(1)} fusion(bf16[8192,224]{0,1:T(8,128)(2,1)} %bitcast.152, f32[8192]{0:T(1024)S(1)} %get-tuple-element.415, s32[8192]{0:T(1024)S(1)} %get-tuple-element.417, f32[8192]{0:T(1024)S(1)} %get-tuple-element.418, s32[8192]{0:T(1024)S(1)} %get-tuple-element.419, f32[8192]{0:T(1024)S(1)} %get-tuple-element.420, ...), kind=kOutput, calls=%fused_computation.17.clone.2 | convolution fusion | flops 482402304 | bytes 4161537 | tf_op jit(solution)/shard_map/while/body/eval_jaxpr/rk,ra->ka/dot_general | solution.py:152
  231.0 18.3 %fusion.102 = f32[224,128]{1,0:T(8,128)S(1)} fusion(bf16[8192,224]{0,1:T(8,128)(2,1)} %bitcast.152, f32[8192]{0:T(1024)S(1)} %get-tuple-element.415, s32[8192]{0:T(1024)S(1)} %get-tuple-element.417, f32[8192]{0:T(1024)S(1)} %get-tuple-element.418, s32[8192]{0:T(1024)S(1)} %get-tuple-element.419, f32[8192]{0:T(1024)S(1)} %get-tuple-element.420, ...), kind=kOutput, calls=%fused_computation.17.clone.2 | convolution fusion | flops 482402304 | bytes 4161537 | tf_op jit(solution)/shard_map/while/body/eval_jaxpr/rk,ra->ka/dot_general | solution.py:152
  254.4 18.3 %fusion.102 = f32[224,128]{1,0:T(8,128)S(1)} fusion(bf16[8192,224]{0,1:T(8,128)(2,1)} %bitcast.152, f32[8192]{0:T(1024)S(1)} %get-tuple-element.415, s32[8192]{0:T(1024)S(1)} %get-tuple-element.417, f32[8192]{0:T(1024)S(1)} %get-tuple-element.418, s32[8192]{0:T(1024)S(1)} %get-tuple-element.419, f32[8192]{0:T(1024)S(1)} %get-tuple-element.420, ...), kind=kOutput, calls=%fused_computation.17.clone.2 | convolution fusion | flops 482402304 | bytes 4161537 | tf_op jit(solution)/shard_map/while/body/eval_jaxpr/rk,ra->ka/dot_general | solution.py:152
  277.8 18.3 %fusion.102 = f32[224,128]{1,0:T(8,128)S(1)} fusion(bf16[8192,224]{0,1:T(8,128)(2,1)} %bitcast.152, f32[8192]{0:T(1024)S(1)} %get-tuple-element.415, s32[8192]{0:T(1024)S(1)} %get-tuple-element.417, f32[8192]{0:T(1024)S(1)} %get-tuple-element.418, s32[8192]{0:T(1024)S(1)} %get-tuple-element.419, f32[8192]{0:T(1024)S(1)} %get-tuple-element.420, ...), kind=kOutput, calls=%fused_computation.17.clone.2 | convolution fusion | flops 482402304 | bytes 4161537 | tf_op jit(solution)/shard_map/while/body/eval_jaxpr/rk,ra->ka/dot_general | solution.py:152
  301.2 18.3 %fusion.102 = f32[224,128]{1,0:T(8,128)S(1)} fusion(bf16[8192,224]{0,1:T(8,128)(2,1)} %bitcast.152, f32[8192]{0:T(1024)S(1)} %get-tuple-element.415, s32[8192]{0:T(1024)S(1)} %get-tuple-element.417, f32[8192]{0:T(1024)S(1)} %get-tuple-element.418, s32[8192]{0:T(1024)S(1)} %get-tuple-element.419, f32[8192]{0:T(1024)S(1)} %get-tuple-element.420, ...), kind=kOutput, calls=%fused_computation.17.clone.2 | convolution fusion | flops 482402304 | bytes 4161537 | tf_op jit(solution)/shard_map/while/body/eval_jaxpr/rk,ra->ka/dot_general | solution.py:152
  324.6 18.3 %fusion.102 = f32[224,128]{1,0:T(8,128)S(1)} fusion(bf16[8192,224]{0,1:T(8,128)(2,1)} %bitcast.152, f32[8192]{0:T(1024)S(1)} %get-tuple-element.415, s32[8192]{0:T(1024)S(1)} %get-tuple-element.417, f32[8192]{0:T(1024)S(1)} %get-tuple-element.418, s32[8192]{0:T(1024)S(1)} %get-tuple-element.419, f32[8192]{0:T(1024)S(1)} %get-tuple-element.420, ...), kind=kOutput, calls=%fused_computation.17.clone.2 | convolution fusion | flops 482402304 | bytes 4161537 | tf_op jit(solution)/shard_map/while/body/eval_jaxpr/rk,ra->ka/dot_general | solution.py:152
  348.0 18.3 %fusion.102 = f32[224,128]{1,0:T(8,128)S(1)} fusion(bf16[8192,224]{0,1:T(8,128)(2,1)} %bitcast.152, f32[8192]{0:T(1024)S(1)} %get-tuple-element.415, s32[8192]{0:T(1024)S(1)} %get-tuple-element.417, f32[8192]{0:T(1024)S(1)} %get-tuple-element.418, s32[8192]{0:T(1024)S(1)} %get-tuple-element.419, f32[8192]{0:T(1024)S(1)} %get-tuple-element.420, ...), kind=kOutput, calls=%fused_computation.17.clone.2 | convolution fusion | flops 482402304 | bytes 4161537 | tf_op jit(solution)/shard_map/while/body/eval_jaxpr/rk,ra->ka/dot_general | solution.py:152
  371.4 18.3 %fusion.102 = f32[224,128]{1,0:T(8,128)S(1)} fusion(bf16[8192,224]{0,1:T(8,128)(2,1)} %bitcast.152, f32[8192]{0:T(1024)S(1)} %get-tuple-element.415, s32[8192]{0:T(1024)S(1)} %get-tuple-element.417, f32[8192]{0:T(1024)S(1)} %get-tuple-element.418, s32[8192]{0:T(1024)S(1)} %get-tuple-element.419, f32[8192]{0:T(1024)S(1)} %get-tuple-element.420, ...), kind=kOutput, calls=%fused_computation.17.clone.2 | convolution fusion | flops 482402304 | bytes 4161537 | tf_op jit(solution)/shard_map/while/body/eval_jaxpr/rk,ra->ka/dot_general | solution.py:152
  394.8 18.3 %fusion.102 = f32[224,128]{1,0:T(8,128)S(1)} fusion(bf16[8192,224]{0,1:T(8,128)(2,1)} %bitcast.152, f32[8192]{0:T(1024)S(1)} %get-tuple-element.415, s32[8192]{0:T(1024)S(1)} %get-tuple-element.417, f32[8192]{0:T(1024)S(1)} %get-tuple-element.418, s32[8192]{0:T(1024)S(1)} %get-tuple-element.419, f32[8192]{0:T(1024)S(1)} %get-tuple-element.420, ...), kind=kOutput, calls=%fused_computation.17.clone.2 | convolution fusion | flops 482402304 | bytes 4161537 | tf_op jit(solution)/shard_map/while/body/eval_jaxpr/rk,ra->ka/dot_general | solution.py:152
  418.2 18.3 %fusion.102 = f32[224,128]{1,0:T(8,128)S(1)} fusion(bf16[8192,224]{0,1:T(8,128)(2,1)} %bitcast.152, f32[8192]{0:T(1024)S(1)} %get-tuple-element.415, s32[8192]{0:T(1024)S(1)} %get-tuple-element.417, f32[8192]{0:T(1024)S(1)} %get-tuple-element.418, s32[8192]{0:T(1024)S(1)} %get-tuple-element.419, f32[8192]{0:T(1024)S(1)} %get-tuple-element.420, ...), kind=kOutput, calls=%fused_computation.17.clone.2 | convolution fusion | flops 482402304 | bytes 4161537 | tf_op jit(solution)/shard_map/while/body/eval_jaxpr/rk,ra->ka/dot_general | solution.py:152
  441.6 18.3 %fusion.102 = f32[224,128]{1,0:T(8,128)S(1)} fusion(bf16[8192,224]{0,1:T(8,128)(2,1)} %bitcast.152, f32[8192]{0:T(1024)S(1)} %get-tuple-element.415, s32[8192]{0:T(1024)S(1)} %get-tuple-element.417, f32[8192]{0:T(1024)S(1)} %get-tuple-element.418, s32[8192]{0:T(1024)S(1)} %get-tuple-element.419, f32[8192]{0:T(1024)S(1)} %get-tuple-element.420, ...), kind=kOutput, calls=%fused_computation.17.clone.2 | convolution fusion | flops 482402304 | bytes 4161537 | tf_op jit(solution)/shard_map/while/body/eval_jaxpr/rk,ra->ka/dot_general | solution.py:152
  465.0 18.3 %fusion.102 = f32[224,128]{1,0:T(8,128)S(1)} fusion(bf16[8192,224]{0,1:T(8,128)(2,1)} %bitcast.152, f32[8192]{0:T(1024)S(1)} %get-tuple-element.415, s32[8192]{0:T(1024)S(1)} %get-tuple-element.417, f32[8192]{0:T(1024)S(1)} %get-tuple-element.418, s32[8192]{0:T(1024)S(1)} %get-tuple-element.419, f32[8192]{0:T(1024)S(1)} %get-tuple-element.420, ...), kind=kOutput, calls=%fused_computation.17.clone.2 | convolution fusion | flops 482402304 | bytes 4161537 | tf_op jit(solution)/shard_map/while/body/eval_jaxpr/rk,ra->ka/dot_general | solution.py:152
  488.4 18.3 %fusion.102 = f32[224,128]{1,0:T(8,128)S(1)} fusion(bf16[8192,224]{0,1:T(8,128)(2,1)} %bitcast.152, f32[8192]{0:T(1024)S(1)} %get-tuple-element.415, s32[8192]{0:T(1024)S(1)} %get-tuple-element.417, f32[8192]{0:T(1024)S(1)} %get-tuple-element.418, s32[8192]{0:T(1024)S(1)} %get-tuple-element.419, f32[8192]{0:T(1024)S(1)} %get-tuple-element.420, ...), kind=kOutput, calls=%fused_computation.17.clone.2 | convolution fusion | flops 482402304 | bytes 4161537 | tf_op jit(solution)/shard_map/while/body/eval_jaxpr/rk,ra->ka/dot_general | solution.py:152
  511.8 18.3 %fusion.102 = f32[224,128]{1,0:T(8,128)S(1)} fusion(bf16[8192,224]{0,1:T(8,128)(2,1)} %bitcast.152, f32[8192]{0:T(1024)S(1)} %get-tuple-element.415, s32[8192]{0:T(1024)S(1)} %get-tuple-element.417, f32[8192]{0:T(1024)S(1)} %get-tuple-element.418, s32[8192]{0:T(1024)S(1)} %get-tuple-element.419, f32[8192]{0:T(1024)S(1)} %get-tuple-element.420, ...), kind=kOutput, calls=%fused_computation.17.clone.2 | convolution fusion | flops 482402304 | bytes 4161537 | tf_op jit(solution)/shard_map/while/body/eval_jaxpr/rk,ra->ka/dot_general | solution.py:152
  535.2 18.3 %fusion.102 = f32[224,128]{1,0:T(8,128)S(1)} fusion(bf16[8192,224]{0,1:T(8,128)(2,1)} %bitcast.152, f32[8192]{0:T(1024)S(1)} %get-tuple-element.415, s32[8192]{0:T(1024)S(1)} %get-tuple-element.417, f32[8192]{0:T(1024)S(1)} %get-tuple-element.418, s32[8192]{0:T(1024)S(1)} %get-tuple-element.419, f32[8192]{0:T(1024)S(1)} %get-tuple-element.420, ...), kind=kOutput, calls=%fused_computation.17.clone.2 | convolution fusion | flops 482402304 | bytes 4161537 | tf_op jit(solution)/shard_map/while/body/eval_jaxpr/rk,ra->ka/dot_general | solution.py:152
  558.6 18.3 %fusion.102 = f32[224,128]{1,0:T(8,128)S(1)} fusion(bf16[8192,224]{0,1:T(8,128)(2,1)} %bitcast.152, f32[8192]{0:T(1024)S(1)} %get-tuple-element.415, s32[8192]{0:T(1024)S(1)} %get-tuple-element.417, f32[8192]{0:T(1024)S(1)} %get-tuple-element.418, s32[8192]{0:T(1024)S(1)} %get-tuple-element.419, f32[8192]{0:T(1024)S(1)} %get-tuple-element.420, ...), kind=kOutput, calls=%fused_computation.17.clone.2 | convolution fusion | flops 482402304 | bytes 4161537 | tf_op jit(solution)/shard_map/while/body/eval_jaxpr/rk,ra->ka/dot_general | solution.py:152
  599.1 35.5 %all-gather.3.cloned.1.call-done = f32[32,4,32,128]{3,2,1,0:T(8,128)} async-done(((f32[4,4,32,128]{3,2,1,0:T(8,128)}), f32[32,4,32,128]{3,2,1,0:T(8,128)}) %all-gather.3.cloned.1.call-update) | async-done | bytes 2097168 | tf_op jit(solution)/shard_map/all_gather | solution.py:28
  634.6 23.8 %all-gather.5.cloned.1.call-done = f32[64,4,32,128]{3,2,1,0:T(8,128)} async-done(((f32[32,4,32,128]{3,2,1,0:T(8,128)}), f32[64,4,32,128]{3,2,1,0:T(8,128)}) %all-gather.5.cloned.1.call-update) | async-done | bytes 4194320 | tf_op jit(solution)/shard_map/all_gather | solution.py:28
  672.5 14.7 %all-to-all-done.1 = f32[4,256,2,128]{3,1,2,0:T(8,128)S(1)} async-done(((f32[4,256,2,128]{3,1,2,0:T(8,128)}), f32[4,256,2,128]{3,1,2,0:T(8,128)S(1)}, u32[]{:S(2)}, u32[]{:S(2)}) %all-to-all-start.1) | async-done | bytes 1048608 | tf_op jit(solution)/shard_map/all_to_all | solution.py:41
  (289 shorter events, 161.6 us)
Async XLA Ops:
  7.2 6.3 copy-start.1
  7.2 6.3 copy-start.2
  67.9 107.8 %all-to-all-start = ((f32[7,64,2048]{2,0,1:T(8,128)}), f32[7,64,2048]{2,0,1:T(8,128)}, u32[]{:S(2)}, u32[]{:S(2)}) async-start(f32[7,64,2048]{2,0,1:T(8,128)} %bitcast.153), calls=%async_computation | async-start | bytes 8388608 | tf_op jit(solution)/shard_map/all_to_all | solution.py:135
  81.2 553.4 %all-gather.3.cloned.1.call-start = ((), (), s32[]{:S(2)}) async-start(), calls=%async_computation.2 | async-start | bytes 2359296 | tf_op jit(solution)/shard_map/all_gather | solution.py:28
  576.9 7.2 collective-permute-start
  582.2 5.1 collective-permute-start.1
  598.9 59.5 %all-gather.5.cloned.1.call-start = ((), (), s32[]{:S(2)}) async-start(), calls=%async_computation.3 | async-start | bytes 6291456 | tf_op jit(solution)/shard_map/all_gather | solution.py:28
  668.7 18.7 %copy-start.3 = (f32[16]{0:T(128)S(1)}, f32[16]{0:T(128)}, u32[]{:S(2)}) copy-start(f32[16]{0:T(128)} %param.27) | copy-start | bytes 196
  668.7 18.5 %all-to-all-start.1 = ((f32[4,256,2,128]{3,1,2,0:T(8,128)}), f32[4,256,2,128]{3,1,2,0:T(8,128)S(1)}, u32[]{:S(2)}, u32[]{:S(2)}) async-start(f32[4,256,2,128]{3,1,2,0:T(8,128)} %broadcast_in_dim.224), calls=%async_computation.1 | async-start | bytes 2097152 | tf_op jit(solution)/shard_map/all_to_all | solution.py:41
  691.5 2.2 copy-start
  691.5 2.2 copy-start.4
  691.5 2.2 copy-start.5
Sparse Core Ops, SparseCore 0:
  599.0 35.5 all-gather.2
  636.4 21.9 all-gather.4
where the time goes:
time: 725 us; the launch traced here: 721 us
  matrix products  293 us (40%)
  waiting for transfers between devices  171 us (24%)
  local copies, waits for them, and re-layouts  108 us (15%)
  other arithmetic  97.7 us (13%)
  starting transfers between devices  24.8 us (3%)
  between operations  14.4 us (2%)
  blocking collectives  11.6 us (2%)
    dot_general x16, matrix products, owner_step(): jnp.einsum('rk,ra->ka', left, age_table, preferred_element_type=jnp.float32)  293 us
    all_to_all x1, waiting for transfers between devices, per_device(): lax.all_to_all(outgoing.reshape(7, tiles, capacity * 128), TILE, split_ax...  94.2 us
    all_gather x2, waiting for transfers between devices, all_blocks(): parts = lax.all_gather(parts, axes[k], axis=0, tiled=True)  59.3 us
    scatter x1, local copies, waits for them, and re-layouts, per_device(): jnp.zeros((7, tiles * capacity, 128), jnp.float32).at[:, target].set(packed)  47.4 us
    convert_element_type x16, other arithmetic, factors(): (scaled[:, :, :, None] * onehot[:, None, None, :]).astype(jnp.bfloat16)  38.4 us
    slice x1, local copies, waits for them, and re-layouts, per_device(): arrived[index]  22.5 us
    convert_element_type x16, other arithmetic, owner_step(): item[1].astype(jnp.int32)  16.2 us
    dynamic_slice x16, local copies, waits for them, and re-layouts, per_device(): lax.scan(owner_step, initial, tuple((arrived[index] for index in range(7))))  15.7 us
  transfers between devices with their start and end apart: 6, of which 5 were waited for; matrix products, arithmetic and copies ran while one was open for 0% of the time, Pallas kernels for 0%

commit v1 on v0

v1 whole, which is shorter than its diff:
```python
import jax, jax.numpy as jnp
from jax import lax
from jax.experimental import pallas as pl
from jax.experimental.pallas import tpu as pltpu
from jax.sharding import Mesh
from jax.sharding import PartitionSpec as P

ITERS = 4
MESH = pl.DeviceIdType.MESH
F32, BF16, I32 = jnp.float32, jnp.bfloat16, jnp.int32

def spline(f):
    r = 1.0 - f
    f2 = f * f
    c = f2 * f
    s = 1.0 / 6.0
    return (r * r * r * s, (3.0 * c - 6.0 * f2 + 4.0) * s, (-3.0 * c + 3.0 * f2 + 3.0 * f + 1.0) * s, c * s)

def grid_kernel(tile_ref, age_ref, dur_ref, code_ref, af_ref, df_ref, ex_ref, cl_ref, out_ref, acc):
    acc[...] = jnp.zeros(acc.shape, F32)
    iota8 = lax.broadcasted_iota(I32, (8, 128), 0)
    iota16 = lax.broadcasted_iota(I32, (16, 128), 0)
    half16 = (iota16 >> 3).astype(F32).astype(BF16)
    zero16 = jnp.zeros((16, 128), BF16)
    r1 = iota16 + 1

    def group(g, _):
        base = pl.multiple_of(g * 8, 8)
        at = pl.ds(base, 8)
        aw = spline(af_ref[at, :])
        dw = spline(df_ref[at, :])
        age, dc = age_ref[at, :], dur_ref[at, :]
        code = code_ref[at, :].astype(F32)
        ex, cl = ex_ref[at, :], cl_ref[at, :]
        for i in range(8):
            def row(x, n):
                return jnp.broadcast_to(x[i : i + 1, :], (n, 128))
            delta = iota8 - row(dc, 8)
            w = jnp.where(delta == 0, row(dw[0], 8), 0.0)
            for k in range(1, 4):
                w = jnp.where(delta == k, row(dw[k], 8), w)
            e = w * row(ex, 8)
            c = w * row(cl, 8)
            e16 = jnp.concatenate([e, e], 0).astype(BF16)
            c16 = jnp.concatenate([c, c], 0).astype(BF16)
            code16 = row(code, 16).astype(BF16)
            le, lc = [], []
            rel = code16 - half16
            for j in range(8):
                m = rel == jnp.bfloat16(2 * j)
                le.append(jnp.where(m, e16, zero16))
                lc.append(jnp.where(m, c16, zero16))
            lhs = jnp.concatenate(le + lc, 0)
            ageb = row(age, 16)
            kk = (r1 - ageb) & 15
            a = jnp.where(kk == 0, row(aw[0], 16), 0.0)
            for k in range(1, 4):
                a = jnp.where(kk == k, row(aw[k], 16), a)
            a16 = a.astype(BF16)
            grp = ((ageb - 1 + kk) >> 4).astype(F32).astype(BF16)
            rhs = jnp.concatenate([jnp.where(grp == jnp.bfloat16(q), a16, zero16) for q in range(8)], 0)
            res = lax.dot_general(lhs, rhs, (((1,), (1,)), ((), ())), preferred_element_type=F32)
            tile = tile_ref[g * 8 + i]
            idx = (tile & 1) * 32 + (tile >> 1)
            acc[idx] += res
        return 0

    lax.fori_loop(0, 64, group, 0)

    sub = lax.broadcasted_iota(I32, (8, 128), 0)

    def comb(m, _):
        h = m // 16
        s = (m % 16) // 8
        r8 = pl.multiple_of((m % 8) * 8, 8)
        up = jnp.minimum(m + 1, 31)
        dn = jnp.maximum(m - 1, 0)
        pooled = [jnp.zeros((8, 128), F32), jnp.zeros((8, 128), F32)]
        for ch in range(2):
            for t in range(16):
                ct = ch * 16 + t
                sl = pl.ds(ct * 8, 8)
                ev = jnp.where(sub == 0, acc[up, sl, :], acc[m, sl, :])
                ev = jnp.where((sub == 0) & (m == 31), 0.0, ev)
                ev = pltpu.roll(ev, 7, 0)
                od = jnp.where(sub >= 5, acc[32 + dn, sl, :], acc[32 + m, sl, :])
                od = jnp.where((sub >= 5) & (m == 0), 0.0, od)
                od = pltpu.roll(od, 3, 0)
                v = ev + od
                pooled[ch] = pooled[ch] + v
                z, y = t >> 1, 2 * (t & 1) + s
                slot = jnp.where(h == 0, y * 8 + z, z * 4 + y)
                out_ref[h, slot, pl.ds(ch * 64 + r8, 8), :] = v
        pe, po = pooled
        low = sub < 4
        z, y = m // 4, m % 4
        out_ref[0, y * 8 + z, 128:136, :] = jnp.where(low, pe, pltpu.roll(po, 4, 0))
        out_ref[1, z * 4 + y, 128:136, :] = jnp.where(low, pltpu.roll(pe, 4, 0), po)
        return 0

    lax.fori_loop(0, 32, comb, 0)

def grids(tiles, fields):
    n = pl.BlockSpec(memory_space=pltpu.VMEM)
    return pl.pallas_call(
        grid_kernel,
        out_shape=jax.ShapeDtypeStruct((2, 32, 136, 128), F32),
        in_specs=[pl.BlockSpec(memory_space=pltpu.SMEM)] + [n] * 7,
        out_specs=n,
        scratch_shapes=[pltpu.VMEM((64, 256, 128), F32)],
        compiler_params=pltpu.CompilerParams(vmem_limit_bytes=40 << 20),
        cost_estimate=pl.CostEstimate(flops=2*512*256*128*128, bytes_accessed=6<<20, transcendentals=0),
        name="local_grid",
    )(tiles, *fields)


ROWS = 136


def penalty(v, axis):
    n = v.shape[axis]
    place = lax.broadcasted_iota(I32, v.shape, axis)
    u = v - 2.0 * pltpu.roll(v, n - 1, axis) + pltpu.roll(v, n - 2, axis)
    u = jnp.where(place < n - 2, u, 0.0)
    return u - 2.0 * pltpu.roll(u, 1, axis) + pltpu.roll(u, 2, axis)


def chain_order(n):
    order = [(n // 2, 0)]
    for k in range(n // 2 - 1, 0, -1):
        order += [(k, 1), (k, 0)]
    return order


def reduce_along(n, me, neighbour, piece, land, sizes, send_sem, recv_sem, prepare):
    order = chain_order(n)
    started = []

    def copy(way, j):
        k, first = order[j]
        sub = (0 if first == 0 else 1) if way == 0 else (1 if first == 0 else 0)
        dest = lax.rem(me + (k if way == 0 else n - k), n)
        return dest, sub

    def transfer(way, j):
        dest, sub = copy(way, j)
        return pltpu.make_async_remote_copy(
            src_ref=piece(dest, sub),
            dst_ref=land(way, j, sub),
            send_sem=send_sem.at[way, j],
            recv_sem=recv_sem.at[way, j],
            device_id=neighbour(1 if way == 0 else n - 1),
            device_id_type=MESH,
        )

    def take(way, j, dest):
        _, sub = copy(way, j)
        transfer(way, j).wait_recv()
        target = piece(dest, sub)
        target[...] += land(way, j, sub)[...]

    for j, (k, first) in enumerate(order):
        for way in (0, 1):
            dest, sub = copy(way, j)
            prepare(k, way)
            if (k + 1, first) in order:
                take(way, order.index((k + 1, first)), dest)
            move = transfer(way, j)
            move.start()
            started.append(move)
    prepare(0, 0)
    for first in (1, 0):
        for way in (0, 1):
            take(way, order.index((1, first)), me) if (1, first) in order else None
    return started


def smooth_kernel(
    g_ref, age_weight, dur_weight, credibility, out_s, out_r,
    part, other, land1, land2, grid, pool, twin, prior, done, got,
    local_sem, s0_send, s0_recv, s1_send, s1_recv, s2_send, s2_recv,
    ag_send, ag_recv, x_send, x_recv, t_send, t_recv, y_send, y_recv, z_send, z_recv, o_send, o_recv,
):
    x, z, y, c = (lax.axis_index(a) for a in ("tg", "z", "y", "c"))

    barrier = pltpu.get_barrier_semaphore()

    def greet(i, _):
        zz, yy, cc = i // 8, lax.rem(i // 2, 4), lax.rem(i, 2)

        @pl.when(i != z * 8 + y * 2 + c)
        def _():
            pl.semaphore_signal(barrier, inc=1, device_id=(x, zz, yy, cc), device_id_type=MESH)

        return 0

    lax.fori_loop(0, 64, greet, 0)
    for d in range(1, 4):
        pl.semaphore_signal(barrier, inc=1, device_id=(lax.rem(x + d, 4), z, y, c), device_id_type=MESH)
    pl.semaphore_wait(barrier, 66)

    sibling = (x, z, y, 1 - c)

    def along_y(d):
        return (x, z, lax.rem(y + d, 4), c)

    def along_z(d):
        return (x, lax.rem(z + d, 8), y, c)

    def dests(n, i):
        order = [lax.rem(i + n // 2, n)]
        for k in range(n // 2 - 1, 0, -1):
            order += [lax.rem(i + k, n), lax.rem(i + n - k, n)]
        return order + [i]

    def role(core, n, i, first_axis, n2, i2, second_axis):
        many = 32 // n
        half = many // 2
        sib = 1 - core
        sib_n, sib_i = (8, z) if core == 0 else (4, y)
        sib_many = 32 // sib_n
        sends = []
        for j, d in enumerate(dests(sib_n, sib_i)):
            at = pl.ds(d * sib_many, sib_many)
            move = pltpu.make_async_remote_copy(
                src_ref=g_ref.at[sib, at], dst_ref=other.at[at],
                send_sem=s0_send.at[j], recv_sem=s0_recv.at[j],
                device_id=sibling, device_id_type=MESH,
            )
            move.start()
            sends.append(move)
        mine = []
        for j, d in enumerate(dests(n, i)):
            at = pl.ds(d * many, many)
            load = pltpu.make_async_copy(g_ref.at[core, at], part.at[at], local_sem.at[j])
            load.start()
            mine.append((load, at))
        ready = set()

        def prepare(k, way):
            j = 0 if k == n // 2 else (n - 1 if k == 0 else 1 + 2 * (n // 2 - 1 - k) + way)
            if j in ready:
                return
            ready.add(j)
            load, at = mine[j]
            load.wait()
            pltpu.make_async_remote_copy(
                src_ref=g_ref.at[core, at], dst_ref=other.at[at],
                send_sem=s0_send.at[j], recv_sem=s0_recv.at[j],
                device_id=sibling, device_id_type=MESH,
            ).wait_recv()
            part[at] += other[at]

        def piece1(d, sub):
            return part.at[pl.ds(d * many + sub * half, half)]

        def land_1(way, j, sub):
            return land1.at[pl.ds((way * (n - 1) + j) * half, half)]

        sends += reduce_along(n, i, first_axis, piece1, land_1, None, s1_send, s1_recv, prepare)

        def rows(sub):
            return pl.ds(0, 72) if sub == 0 else pl.ds(72, 64)

        def piece2(d, sub):
            return part.at[i * many + d, rows(sub)]

        def land_2(way, j, sub):
            return land2.at[way * 7 + j, pl.ds(0, 72 if sub == 0 else 64)]

        sends += reduce_along(n2, i2, second_axis, piece2, land_2, None, s2_send, s2_recv, lambda k, way: None)

        own = i * many + i2
        quarter = 2 * c + lax.rem(y, 2)
        for d in range(1, 4):
            move = pltpu.make_async_remote_copy(
                src_ref=part.at[own, pl.ds(128, 8)], dst_ref=pool.at[d],
                send_sem=x_send.at[d], recv_sem=x_recv.at[d],
                device_id=(lax.rem(x + d, 4), z, y, c), device_id_type=MESH,
            )
            move.start()
            sends.append(move)
        pair = y + 1 - 2 * lax.rem(y, 2)
        for j, peer in enumerate(((x, z, y, 1 - c), (x, z, pair, c), (x, z, pair, 1 - c))):
            move = pltpu.make_async_remote_copy(
                src_ref=part.at[own, pl.ds(0, 128)], dst_ref=grid.at[quarter],
                send_sem=ag_send.at[j], recv_sem=ag_recv.at[j],
                device_id=peer, device_id_type=MESH,
            )
            move.start()
            sends.append(move)
        grid[quarter] = part[own, 0:128]
        pool[0] = part[own, 128:136]
        for move in sends:
            move.wait_send()

    @pl.when(c == 0)
    def _():
        role(0, 4, y, along_y, 8, z, along_z)

    @pl.when(c == 1)
    def _():
        role(1, 8, z, along_z, 4, y, along_y)

    def arrive(dst, sem, src=None):
        pltpu.make_async_remote_copy(
            src_ref=dst, dst_ref=dst, send_sem=sem, recv_sem=sem, device_id=sibling, device_id_type=MESH
        ).wait_recv()

    sends = []

    def send(src, dst, s, r, peer):
        move = pltpu.make_async_remote_copy(
            src_ref=src, dst_ref=dst, send_sem=s, recv_sem=r, device_id=peer, device_id_type=MESH
        )
        move.start()
        sends.append(move)

    for d in range(1, 4):
        arrive(pool.at[d], x_recv.at[d])
    total = (pool[0] + pool[1]) + (pool[2] + pool[3])
    twin[0] = pltpu.roll(total, 4, 0) / (1.0 + total)
    send(twin.at[0], twin.at[1], t_send.at[0], t_recv.at[0], sibling)
    arrive(twin.at[1], t_recv.at[0])
    low = jnp.where(c == 0, twin[0], twin[1])
    high = jnp.where(c == 0, twin[1], twin[0])
    under = lax.broadcasted_iota(I32, (8, 128), 0) < 4
    prior[z, y] = jnp.where(under, low, pltpu.roll(high, 4, 0))
    for d in range(1, 4):
        send(prior.at[z, y], prior.at[z, y], y_send.at[d], y_recv.at[d], along_y(d))
    for d in range(1, 4):
        arrive(prior.at[z, lax.rem(y + 4 - d, 4)], y_recv.at[d])
    for d in range(1, 8):
        send(prior.at[z], prior.at[z], z_send.at[d], z_recv.at[d], along_z(d))
    for d in range(1, 8):
        arrive(prior.at[lax.rem(z + 8 - d, 8)], z_recv.at[d])
    quarter = 2 * c + lax.rem(y, 2)
    pair = lax.rem(y, 2)
    for j, q in enumerate((2 * (1 - c) + pair, 2 * c + 1 - pair, 2 * (1 - c) + 1 - pair)):
        arrive(grid.at[q], ag_recv.at[j])

    t = 2 * z + y // 2
    wa, wd, cred = age_weight[t], dur_weight[t], credibility[t]
    expo = jnp.concatenate([grid[q, 0:64] for q in range(4)], 0)
    claim = jnp.concatenate([grid[q, 64:128] for q in range(4)], 0)
    diagonal = expo + cred
    residual = claim + cred * prior[...].reshape(256, 128)
    direction = residual
    smoothed = jnp.zeros_like(residual)

    def dot(a, b):
        return jnp.sum(a * b, axis=(0, 1), keepdims=True)

    norm = dot(residual, residual)
    for _ in range(ITERS):
        image = diagonal * direction + wa * penalty(direction, 1) + wd * penalty(direction, 0)
        alpha = norm / dot(direction, image)
        smoothed = smoothed + alpha * direction
        residual = residual - alpha * image
        new = dot(residual, residual)
        direction = residual + (new / norm) * direction
        norm = new
    done[:, 0] = smoothed.reshape(32, 8, 128)
    done[:, 1] = residual.reshape(32, 8, 128)

    chip = z * 4 + y
    for j in range(16):
        m = quarter * 8 + j // 2
        self_ = (m == chip) & (j % 2 == c)

        @pl.when(jnp.logical_not(self_))
        def _():
            pltpu.make_async_remote_copy(
                src_ref=done.at[m], dst_ref=got.at[t], send_sem=o_send.at[j], recv_sem=o_recv.at[t],
                device_id=(x, m // 4, lax.rem(m, 4), j % 2), device_id_type=MESH,
            ).start()

    mine = z // 2 == quarter

    @pl.when(mine)
    def _():
        got[t] = done[chip]

    for tt in range(16):
        @pl.when(jnp.logical_not(mine & (t == tt)))
        def _():
            arrive(got.at[tt], o_recv.at[tt])

    for tt in range(16):
        for k, out in enumerate((out_s, out_r)):
            v = got[tt, k]
            v = jnp.where(c == 0, v, pltpu.roll(v, 4, 0))
            out[tt] = v[0:4]
    for move in sends:
        move.wait_send()
    for j in range(16):
        m = quarter * 8 + j // 2

        @pl.when(jnp.logical_not((m == chip) & (j % 2 == c)))
        def _():
            pltpu.make_async_remote_copy(
                src_ref=done.at[m], dst_ref=got.at[t], send_sem=o_send.at[j], recv_sem=o_recv.at[t],
                device_id=sibling, device_id_type=MESH,
            ).wait_send()


def smooth(parts, smooth_age, smooth_dur, credibility):
    smem = pl.BlockSpec(memory_space=pltpu.SMEM)
    vmem = pl.BlockSpec(memory_space=pltpu.VMEM)
    dma = pltpu.SemaphoreType.DMA
    return pl.pallas_call(
        smooth_kernel,
        out_shape=(jax.ShapeDtypeStruct((16, 4, 128), F32),) * 2,
        in_specs=[pl.BlockSpec(memory_space=pl.ANY), smem, smem, smem],
        out_specs=(vmem, vmem),
        scratch_shapes=[
            pltpu.VMEM((32, ROWS, 128), F32),
            pltpu.VMEM((32, ROWS, 128), F32),
            pltpu.VMEM((28, ROWS, 128), F32),
            pltpu.VMEM((14, 72, 128), F32),
            pltpu.VMEM((4, 128, 128), F32),
            pltpu.VMEM((4, 8, 128), F32),
            pltpu.VMEM((2, 8, 128), F32),
            pltpu.VMEM((8, 4, 8, 128), F32),
            pltpu.VMEM((32, 2, 8, 128), F32),
            pltpu.VMEM((16, 2, 8, 128), F32),
            dma((8,)), dma((8,)), dma((8,)),
            dma((2, 7)), dma((2, 7)), dma((2, 7)), dma((2, 7)),
            dma((3,)), dma((3,)), dma((4,)), dma((4,)), dma((1,)), dma((1,)),
            dma((4,)), dma((4,)), dma((8,)), dma((8,)), dma((16,)), dma((16,)),
        ],
        compiler_params=pltpu.CompilerParams(collective_id=0, has_side_effects=True, vmem_limit_bytes=40 << 20),
        cost_estimate=pl.CostEstimate(flops=20 << 20, bytes_accessed=6 << 20, transcendentals=0),
        name="reduce_and_smooth",
    )(parts, smooth_age, smooth_dur, credibility)


def per_device(
    age_cell, dur_cell, trans_code, age_frac, dur_frac, exposure, claims, block_tile, smooth_age, smooth_dur, credibility
):
    fields = [
        f.reshape(-1, 128) for f in (age_cell, dur_cell, trans_code, age_frac, dur_frac, exposure, claims)
    ]
    parts = grids(block_tile.reshape(-1), fields)
    return smooth(parts, smooth_age, smooth_dur, credibility)


def solution(mesh):
    split = Mesh(mesh.devices.reshape(mesh.shape["tg"], 8, 4, 2), ("tg", "z", "y", "c"))
    tile = ("z", "y", "c")
    placed = (P("tg", tile),) * 7 + (P("tg", tile, None),) + (P("tg"),) * 3
    return jax.shard_map(
        per_device,
        mesh=split,
        in_specs=placed,
        out_specs=(P("tg", tile, None),) * 2,
        check_vma=False,
    )
```

time: 725 us -> 96.9 us (0.13)
  matrix products: 293 us -> 0 us
  waiting for transfers between devices: 171 us -> 0 us
  local copies, waits for them, and re-layouts: 108 us -> 8.56 us
  other arithmetic: 97.7 us -> 0 us
  Pallas kernels: 0 us -> 87.3 us
  starting transfers between devices: 24.8 us -> 0 us
  between operations: 14.4 us -> 0.69 us
  blocking collectives: 11.6 us -> 0 us
    dot_general x16 -> x0, matrix products: 293 us -> none  [owner_step(): jnp.einsum('rk,ra->ka', left, age_table, preferred_element_type=jnp.float32)]
    all_to_all x2 -> x0, waiting for transfers between devices: 109 us -> none  [the longest x1 94.2 us: per_device(): lax.all_to_all(outgoing.reshape(7, tiles, capacity * 128), TILE, split_ax...]
    pallas_call x0 -> x2, Pallas kernels: none -> 87.3 us  [the longest x1 62.9 us: smooth(): pl.pallas_call(smooth_kernel, out_shape=(jax.ShapeDtypeStruct((16, 4, 128...]
    convert_element_type x67 -> x0, other arithmetic: 59.7 us -> none  [the longest x16 38.4 us: factors(): (scaled[:, :, :, None] * onehot[:, None, None, :]).astype(jnp.bfloat16)]
    all_gather x2 -> x0, waiting for transfers between devices: 59.3 us -> none  [all_blocks(): parts = lax.all_gather(parts, axes[k], axis=0, tiled=True)]
    scatter x1 -> x0, local copies, waits for them, and re-layouts: 47.4 us -> none  [per_device(): jnp.zeros((7, tiles * capacity, 128), jnp.float32).at[:, target].set(packed)]
    slice x4 -> x0, local copies, waits for them, and re-layouts: 22.5 us -> none  [the longest x1 22.5 us: per_device(): arrived[index]]
    all_to_all x2 -> x0, starting transfers between devices: 17.2 us -> none  [the longest x1 13.3 us: per_device(): lax.all_to_all(outgoing.reshape(7, tiles, capacity * 128), TILE, split_ax...]
  transfers between devices with their start and end apart: 6 -> 0, of which waited for: 5 -> 0; matrix products, arithmetic and copies ran while one was open for 0% -> 0% of each run, Pallas kernels for 0% -> 0%
where the time goes in v1:
time: 96.9 us; the launch traced here: 96.5 us
  Pallas kernels  87.3 us (90%)
  local copies, waits for them, and re-layouts  8.56 us (9%)
    pallas_call x1, Pallas kernels, smooth(): pl.pallas_call(smooth_kernel, out_shape=(jax.ShapeDtypeStruct((16, 4, 128...  62.9 us
    pallas_call x1, Pallas kernels, grids(): pl.pallas_call(grid_kernel, out_shape=jax.ShapeDtypeStruct((2, 32, 136, 1...  24.4 us
    unnamed x24, local copies, waits for them, and re-layouts  8.56 us

profile of v1, /device:TPU:1, one launch (start us, length us, event | category | flops | bytes accessed | tf_op | source)
XLA Modules:
  0.0 96.5 jit_solution(2492582936027934958)
XLA Ops:
  0.6 0.0 copy-start.3
  0.6 0.9 copy-done.3
  1.6 0.9 copy-done.4
  2.5 0.0 copy-start.5
  2.5 0.9 copy-done.5
  3.5 0.0 copy-start.6
  3.5 0.9 copy-done.6
  4.4 0.0 copy-start.7
  4.4 0.9 copy-done.7
  5.4 0.0 copy-start.8
  5.4 0.9 copy-done.8
  6.3 0.0 copy-start.9
  6.3 0.9 copy-done.9
  7.3 0.0 copy-start.10
  7.3 0.7 copy-done.10
  8.0 0.0 copy-start
  8.0 0.0 copy-start.1
  8.0 24.4 %local_grid.1.g_ref = f32[2,32,136,128]{3,2,1,0:T(8,128)S(1)} custom-call(s32[512]{0:T(512)S(1)} %bitcast.15, s32[512,128]{1,0:T(8,128)S(1)} %bitcast.8, s32[512,128]{1,0:T(8,128)S(1)} %bitcast.9, s32[512,128]{1,0:T(8,128)S(1)} %bitcast.10, f32[512,128]{1,0:T(8,128)S(1)} %bitcast.11, f32[512,128]{1,0:T(8,128)S(1)} %bitcast.12, f32[512,128]{1,0:T(8,128)S(1)} %bitcast.13, ...), custom_call_target="tpu_custom_call" | custom-call | flops 4294967296 | bytes 6291456 | tf_op jit(solution)/shard_map/local_grid/pallas_call | solution.py:105
  32.4 0.0 copy-done
  32.4 0.0 copy-done.1
  32.4 0.0 copy-done.2
  32.4 62.9 %reduce_and_smooth.1 = (f32[16,4,128]{2,1,0:T(4,128)S(1)}, f32[16,4,128]{2,1,0:T(4,128)S(1)}) custom-call(f32[2,32,136,128]{3,2,1,0:T(8,128)S(1)} %local_grid.1.g_ref, f32[16]{0:T(128)S(1)} %copy-done, f32[16]{0:T(128)S(1)} %copy-done.1, f32[16]{0:T(128)S(1)} %copy-done.2), custom_call_target="tpu_custom_call" | custom-call | flops 20971520 | bytes 6291456 | tf_op jit(solution)/shard_map/reduce_and_smooth/pallas_call | solution.py:411
  95.3 0.6 copy.15
  95.9 0.6 copy.16
  (2 shorter events, 0.0 us)
Async XLA Ops:
  0.6 1.0 copy-start.3
  1.6 0.9 copy-start.4
  2.5 0.9 copy-start.5
  3.5 0.9 copy-start.6
  4.4 0.9 copy-start.7
  5.4 0.9 copy-start.8
  6.3 0.9 copy-start.9
  7.3 0.7 copy-start.10
  8.0 24.4 %copy-start = (f32[16]{0:T(128)S(1)}, f32[16]{0:T(128)}, u32[]{:S(2)}) copy-start(f32[16]{0:T(128)} %age_weight.1) | copy-start | bytes 196
  8.0 24.4 %copy-start.1 = (f32[16]{0:T(128)S(1)}, f32[16]{0:T(128)}, u32[]{:S(2)}) copy-start(f32[16]{0:T(128)} %dur_weight.1) | copy-start | bytes 196
  8.0 24.4 %copy-start.2 = (f32[16]{0:T(128)S(1)}, f32[16]{0:T(128)}, u32[]{:S(2)}) copy-start(f32[16]{0:T(128)} %credibility.1) | copy-start | bytes 196

commit v2 on v1

v2 whole, which is shorter than its diff:
```python
import jax, jax.numpy as jnp
from jax import lax
from jax.experimental import pallas as pl
from jax.experimental.pallas import tpu as pltpu
from jax.sharding import Mesh
from jax.sharding import PartitionSpec as P

ITERS = 4
MESH = pl.DeviceIdType.MESH
HBM = pltpu.MemorySpace.HBM
F32, BF16, I32 = jnp.float32, jnp.bfloat16, jnp.int32

def spline(f):
    r = 1.0 - f
    f2 = f * f
    c = f2 * f
    s = 1.0 / 6.0
    return (r * r * r * s, (3.0 * c - 6.0 * f2 + 4.0) * s, (-3.0 * c + 3.0 * f2 + 3.0 * f + 1.0) * s, c * s)

def grid_kernel(
    tile_ref, age_hbm, dur_hbm, code_hbm, af_hbm, df_hbm, ex_hbm, cl_hbm, out_ref, pool_ref,
    acc, age_ref, dur_ref, code_ref, af_ref, df_ref, ex_ref, cl_ref, sem,
):
    loads = []
    for part in range(4):
        at = pl.ds(part * 128, 128)
        for k, (src, dst) in enumerate((
            (age_hbm, age_ref), (dur_hbm, dur_ref), (code_hbm, code_ref), (af_hbm, af_ref),
            (df_hbm, df_ref), (ex_hbm, ex_ref), (cl_hbm, cl_ref),
        )):
            loads.append(pltpu.make_async_copy(src.at[at], dst.at[at], sem.at[part, k]))
            loads[-1].start()
    acc[...] = jnp.zeros(acc.shape, F32)
    iota8 = lax.broadcasted_iota(I32, (8, 128), 0)
    iota16 = lax.broadcasted_iota(I32, (16, 128), 0)
    half16 = (iota16 >> 3).astype(F32).astype(BF16)
    zero16 = jnp.zeros((16, 128), BF16)
    r1 = iota16 + 1

    def group(g, _):
        base = pl.multiple_of(g * 8, 8)
        at = pl.ds(base, 8)
        aw = spline(af_ref[at, :])
        dw = spline(df_ref[at, :])
        age, dc = age_ref[at, :], dur_ref[at, :]
        code = code_ref[at, :].astype(F32)
        ex, cl = ex_ref[at, :], cl_ref[at, :]
        for i in range(8):
            def row(x, n):
                return jnp.broadcast_to(x[i : i + 1, :], (n, 128))
            delta = iota8 - row(dc, 8)
            w = jnp.where(delta == 0, row(dw[0], 8), 0.0)
            for k in range(1, 4):
                w = jnp.where(delta == k, row(dw[k], 8), w)
            e = w * row(ex, 8)
            c = w * row(cl, 8)
            e16 = jnp.concatenate([e, e], 0).astype(BF16)
            c16 = jnp.concatenate([c, c], 0).astype(BF16)
            code16 = row(code, 16).astype(BF16)
            le, lc = [], []
            rel = code16 - half16
            for j in range(8):
                m = rel == jnp.bfloat16(2 * j)
                le.append(jnp.where(m, e16, zero16))
                lc.append(jnp.where(m, c16, zero16))
            lhs = jnp.concatenate(le + lc, 0)
            ageb = row(age, 16)
            kk = (r1 - ageb) & 15
            a = jnp.where(kk == 0, row(aw[0], 16), 0.0)
            for k in range(1, 4):
                a = jnp.where(kk == k, row(aw[k], 16), a)
            a16 = a.astype(BF16)
            grp = ((ageb - 1 + kk) >> 4).astype(F32).astype(BF16)
            rhs = jnp.concatenate([jnp.where(grp == jnp.bfloat16(q), a16, zero16) for q in range(8)], 0)
            res = lax.dot_general(lhs, rhs, (((1,), (1,)), ((), ())), preferred_element_type=F32)
            tile = tile_ref[g * 8 + i]
            idx = (tile & 1) * 32 + (tile >> 1)
            acc[idx] += res
        return 0

    for part in range(4):
        for load in loads[part * 7 : part * 7 + 7]:
            load.wait()
        lax.fori_loop(part * 16, part * 16 + 16, group, 0)

    sub = lax.broadcasted_iota(I32, (8, 128), 0)

    def comb(m, _):
        h = m // 16
        s = (m % 16) // 8
        r8 = pl.multiple_of((m % 8) * 8, 8)
        up = jnp.minimum(m + 1, 31)
        dn = jnp.maximum(m - 1, 0)
        pooled = [jnp.zeros((8, 128), F32), jnp.zeros((8, 128), F32)]
        for ch in range(2):
            for t in range(16):
                ct = ch * 16 + t
                sl = pl.ds(ct * 8, 8)
                ev = jnp.where(sub == 0, acc[up, sl, :], acc[m, sl, :])
                ev = jnp.where((sub == 0) & (m == 31), 0.0, ev)
                ev = pltpu.roll(ev, 7, 0)
                od = jnp.where(sub >= 5, acc[32 + dn, sl, :], acc[32 + m, sl, :])
                od = jnp.where((sub >= 5) & (m == 0), 0.0, od)
                od = pltpu.roll(od, 3, 0)
                v = ev + od
                pooled[ch] = pooled[ch] + v
                z, y = t >> 1, 2 * (t & 1) + s
                slot = jnp.where(h == 0, y * 8 + z, z * 4 + y)
                out_ref[h, slot, pl.ds(ch * 64 + r8, 8), :] = v
        pe, po = pooled
        low = sub < 4
        z, y = m // 4, m % 4
        pool_ref[0, y * 8 + z] = jnp.where(low, pe, pltpu.roll(po, 4, 0))
        pool_ref[1, y * 8 + z] = jnp.where(low, pltpu.roll(pe, 4, 0), po)
        return 0

    lax.fori_loop(0, 32, comb, 0)

def grids(tiles, fields):
    vmem = pl.BlockSpec(memory_space=pltpu.VMEM)
    return pl.pallas_call(
        grid_kernel,
        out_shape=(
            jax.ShapeDtypeStruct((2, 32, 128, 128), F32),
            jax.ShapeDtypeStruct((2, 32, 8, 128), F32),
        ),
        in_specs=[pl.BlockSpec(memory_space=pltpu.SMEM)] + [pl.BlockSpec(memory_space=HBM)] * 7,
        out_specs=(vmem, vmem),
        scratch_shapes=[pltpu.VMEM((64, 256, 128), F32)]
        + [pltpu.VMEM((512, 128), I32)] * 3
        + [pltpu.VMEM((512, 128), F32)] * 4
        + [pltpu.SemaphoreType.DMA((4, 7))],
        compiler_params=pltpu.CompilerParams(vmem_limit_bytes=40 << 20),
        cost_estimate=pl.CostEstimate(flops=2 * 512 * 256 * 128 * 128, bytes_accessed=6 << 20, transcendentals=0),
        name="local_grid",
    )(tiles, *fields)


def penalty(v, axis):
    n = v.shape[axis]
    place = lax.broadcasted_iota(I32, v.shape, axis)
    u = v - 2.0 * pltpu.roll(v, n - 1, axis) + pltpu.roll(v, n - 2, axis)
    u = jnp.where(place < n - 2, u, 0.0)
    return u - 2.0 * pltpu.roll(u, 1, axis) + pltpu.roll(u, 2, axis)


def chain_order(n):
    order = [(n // 2, 0)]
    for k in range(n // 2 - 1, 0, -1):
        order += [(k, 1), (k, 0)]
    return order


def reduce_along(n, me, neighbour, piece, land, send_sem, recv_sem, prepare, hook):
    order = chain_order(n)
    started = []

    def half_of(way, j):
        return order[j][1] if way == 0 else 1 - order[j][1]

    def transfer(way, j):
        k, _ = order[j]
        sub = half_of(way, j)
        dest = lax.rem(me + (k if way == 0 else n - k), n)
        return pltpu.make_async_remote_copy(
            src_ref=piece(dest, sub),
            dst_ref=land(way, j),
            send_sem=send_sem.at[way, j],
            recv_sem=recv_sem.at[way, j],
            device_id=neighbour(1 if way == 0 else n - 1),
            device_id_type=MESH,
        )

    def take(way, j, dest):
        transfer(way, j).wait_recv()
        target = piece(dest, half_of(way, j))
        target[...] += land(way, j)[...]

    for j, (k, first) in enumerate(order):
        for way in (0, 1):
            prepare(k, way)
            if (k + 1, first) in order:
                take(way, order.index((k + 1, first)), lax.rem(me + (k if way == 0 else n - k), n))
            move = transfer(way, j)
            move.start()
            started.append(move)
        hook(j)
    prepare(0, 0)
    for first in (1, 0):
        for way in (0, 1):
            take(way, order.index((1, first)), me)
    return started


def smooth_kernel(
    g_ref, p_ref, age_weight, dur_weight, credibility, out_s, out_r,
    part, other, land1, land2, grid, pool_in, pool_part, pool_y, pool_z, pool_zin, pool, twin, prior, field, done, got,
    local_sem, s0_send, s0_recv, s1_send, s1_recv, s2_send, s2_recv, ag_send, ag_recv,
    pa_send, pa_recv, pb_send, pb_recv, pc_send, pc_recv, x_send, x_recv, t_send, t_recv,
    y_send, y_recv, z_send, z_recv, o_send, o_recv,
):
    x, z, y, c = (lax.axis_index(a) for a in ("tg", "z", "y", "c"))
    sibling = (x, z, y, 1 - c)
    side = lax.rem(y, 2)
    pair = y + 1 - 2 * side

    def along_y(d):
        return (x, z, lax.rem(y + d, 4), c)

    def along_z(d):
        return (x, lax.rem(z + d, 8), y, c)

    def along_x(d):
        return (lax.rem(x + d, 4), z, y, c)

    barrier = pltpu.get_barrier_semaphore()
    peers = [sibling, (x, z, pair, 1 - c)]
    peers += [along_y(d) for d in range(1, 4)] + [along_z(d) for d in range(1, 8)] + [along_x(d) for d in range(1, 4)]
    for peer in peers:
        pl.semaphore_signal(barrier, inc=1, device_id=peer, device_id_type=MESH)
    pl.semaphore_wait(barrier, len(peers))

    def dests(n, i):
        order = [lax.rem(i + n // 2, n)]
        for k in range(n // 2 - 1, 0, -1):
            order += [lax.rem(i + k, n), lax.rem(i + n - k, n)]
        return order + [i]

    def arrive(dst, sem):
        pltpu.make_async_remote_copy(
            src_ref=dst, dst_ref=dst, send_sem=sem, recv_sem=sem, device_id=sibling, device_id_type=MESH
        ).wait_recv()

    def role(core, n, i, first_axis, n2, i2, second_axis, points):
        many = 32 // n
        half = many // 2
        sends = []

        def send(src, dst, s, r, peer):
            move = pltpu.make_async_remote_copy(
                src_ref=src, dst_ref=dst, send_sem=s, recv_sem=r, device_id=peer, device_id_type=MESH
            )
            move.start()
            sends.append(move)

        def pool_to_sibling():
            send(p_ref.at[1 - core], pool_in, pa_send.at[0], pa_recv.at[0], sibling)
            own = pltpu.make_async_copy(p_ref.at[core], pool_part, local_sem.at[8])
            own.start()
            return own

        def pool_along_y():
            pool_own.wait()
            arrive(pool_in, pa_recv.at[0])
            pool_part[...] += pool_in[...]
            for d in (2, 1, 3):
                at = pl.ds(lax.rem(y + d, 4) * 8, 8)
                send(pool_part.at[at], pool_y.at[d], pb_send.at[d], pb_recv.at[d], along_y(d))

        def pool_along_z():
            for d in range(1, 4):
                arrive(pool_y.at[d], pb_recv.at[d])
            pool_z[...] = (pool_part[pl.ds(y * 8, 8)] + pool_y[1]) + (pool_y[2] + pool_y[3])
            for d in (4, 3, 5, 2, 6, 1, 7):
                send(pool_z.at[lax.rem(z + d, 8)], pool_zin.at[d], pc_send.at[d], pc_recv.at[d], along_z(d))

        def pool_along_x():
            for d in range(1, 8):
                arrive(pool_zin.at[d], pc_recv.at[d])
            total = pool_z[z]
            for d in range(1, 8):
                total = total + pool_zin[d]
            pool[0] = total
            for d in (2, 1, 3):
                send(pool.at[0], pool.at[d], x_send.at[d], x_recv.at[d], along_x(d))

        def prior_to_sibling():
            for d in range(1, 4):
                arrive(pool.at[d], x_recv.at[d])
            total = (pool[0] + pool[1]) + (pool[2] + pool[3])
            twin[0] = pltpu.roll(total, 4, 0) / (1.0 + total)
            send(twin.at[0], twin.at[1], t_send.at[0], t_recv.at[0], sibling)

        def prior_along_y():
            arrive(twin.at[1], t_recv.at[0])
            low, high = twin[core], twin[1 - core]
            under = lax.broadcasted_iota(I32, (8, 128), 0) < 4
            prior[z, y] = jnp.where(under, low, pltpu.roll(high, 4, 0))
            for d in (2, 1, 3):
                send(prior.at[z, y], prior.at[z, y], y_send.at[d], y_recv.at[d], along_y(d))

        def prior_along_z():
            for d in range(1, 4):
                arrive(prior.at[z, lax.rem(y + 4 - d, 4)], y_recv.at[d])
            for d in (4, 3, 5, 2, 6, 1, 7):
                send(prior.at[z], prior.at[z], z_send.at[d], z_recv.at[d], along_z(d))

        pool_own = pool_to_sibling()
        sib_n, sib_i = (8, z) if core == 0 else (4, y)
        sib_many = 32 // sib_n
        for j, d in enumerate(dests(sib_n, sib_i)):
            at = pl.ds(d * sib_many, sib_many)
            send(g_ref.at[1 - core, at], other.at[at], s0_send.at[j], s0_recv.at[j], sibling)
        mine = []
        for j, d in enumerate(dests(n, i)):
            at = pl.ds(d * many, many)
            load = pltpu.make_async_copy(g_ref.at[core, at], part.at[at], local_sem.at[j])
            load.start()
            mine.append((load, at))
        ready = set()

        def prepare(k, way):
            j = 0 if k == n // 2 else (n - 1 if k == 0 else 1 + 2 * (n // 2 - 1 - k) + way)
            if j in ready:
                return
            ready.add(j)
            load, at = mine[j]
            load.wait()
            arrive(other.at[at], s0_recv.at[j])
            part[at] += other[at]

        def piece(d, sub):
            return part.at[pl.ds(d * many + sub * half, half)]

        def land(way, j):
            return land1.at[pl.ds((way * (n - 1) + j) * half, half)]

        def hook(j):
            if j in points:
                points[j](pool_along_z, pool_along_x, prior_to_sibling)

        pool_along_y()
        sends += reduce_along(n, i, first_axis, piece, land, s1_send, s1_recv, prepare, hook)

        far = sorted(range(1, n2), key=lambda d: -min(d, n2 - d))
        for d in far:
            send(part.at[i * many + lax.rem(i2 + d, n2)], land2.at[d], s2_send.at[d], s2_recv.at[d], second_axis(d))
        prior_along_y()
        quarter = 2 * core + side
        grid[quarter] = part[i * many + i2]
        for d in reversed(far):
            arrive(land2.at[d], s2_recv.at[d])
            grid[quarter] += land2[d]
        for j, peer in enumerate((sibling, (x, z, pair, c), (x, z, pair, 1 - c))):
            send(grid.at[quarter], grid.at[quarter], ag_send.at[j], ag_recv.at[j], peer)
        prior_along_z()
        for d in range(1, 8):
            arrive(prior.at[lax.rem(z + 8 - d, 8)], z_recv.at[d])
        for j, q in enumerate((2 * (1 - core) + side, 2 * core + 1 - side, 2 * (1 - core) + 1 - side)):
            arrive(grid.at[q], ag_recv.at[j])
        for move in sends:
            move.wait_send()

    def nth(k):
        return lambda *steps: steps[k]()

    @pl.when(c == 0)
    def _():
        role(0, 4, y, along_y, 8, z, along_z, {0: nth(0), 1: nth(1), 2: nth(2)})

    @pl.when(c == 1)
    def _():
        role(1, 8, z, along_z, 4, y, along_y, {1: nth(0), 3: nth(1), 5: nth(2)})

    quarter = 2 * c + side
    t = 2 * z + y // 2
    wa, wd, cred = age_weight[t], dur_weight[t], credibility[t]
    expo = jnp.concatenate([grid[q, 0:64] for q in range(4)], 0)
    claim = jnp.concatenate([grid[q, 64:128] for q in range(4)], 0)
    diagonal = expo + cred
    residual = claim + cred * prior[...].reshape(256, 128)
    direction = residual
    smoothed = jnp.zeros_like(residual)

    def dot(a, b):
        return jnp.sum(a * b, axis=(0, 1), keepdims=True)

    norm = dot(residual, residual)
    for _ in range(ITERS):
        image = diagonal * direction + wa * penalty(direction, 1) + wd * penalty(direction, 0)
        alpha = norm / dot(direction, image)
        smoothed = smoothed + alpha * direction
        residual = residual - alpha * image
        new = dot(residual, residual)
        direction = residual + (new / norm) * direction
        norm = new
    field[0] = smoothed
    field[1] = residual

    for j in range(8):
        at = pl.ds(pl.multiple_of(quarter * 64 + j * 8, 8), 8)
        for k in range(2):
            v = field[k, at]
            done[2 * j, k] = v[0:4]
            done[2 * j + 1, k] = v[4:8]

    chip = z * 4 + y

    def result(j):
        m = quarter * 8 + j // 2
        return jnp.logical_not((m == chip) & (j % 2 == c)), pltpu.make_async_remote_copy(
            src_ref=done.at[j], dst_ref=got.at[t], send_sem=o_send.at[j], recv_sem=o_recv.at[t],
            device_id=(x, quarter * 2 + j // 8, (j // 2) % 4, j % 2), device_id_type=MESH,
        )

    for j in range(16):
        away, move = result(j)
        pl.when(away)(move.start)
    here = z // 2 == quarter

    @pl.when(here)
    def _():
        got[t] = done[lax.rem(chip, 8) * 2 + c]

    for tt in range(16):
        @pl.when(jnp.logical_not(here & (t == tt)))
        def _():
            arrive(got.at[tt], o_recv.at[tt])

    out_s[...] = got[:, 0]
    out_r[...] = got[:, 1]
    for j in range(16):
        away, move = result(j)
        pl.when(away)(move.wait_send)


def smooth(parts, pooled, smooth_age, smooth_dur, credibility):
    smem = pl.BlockSpec(memory_space=pltpu.SMEM)
    vmem = pl.BlockSpec(memory_space=pltpu.VMEM)
    whole = pl.BlockSpec(memory_space=pl.ANY)
    dma = pltpu.SemaphoreType.DMA
    return pl.pallas_call(
        smooth_kernel,
        out_shape=(jax.ShapeDtypeStruct((16, 4, 128), F32),) * 2,
        in_specs=[whole, whole, smem, smem, smem],
        out_specs=(vmem, vmem),
        scratch_shapes=[
            pltpu.VMEM((32, 128, 128), F32),
            pltpu.VMEM((32, 128, 128), F32),
            pltpu.VMEM((28, 128, 128), F32),
            pltpu.VMEM((8, 128, 128), F32),
            pltpu.VMEM((4, 128, 128), F32),
            pltpu.VMEM((32, 8, 128), F32),
            pltpu.VMEM((32, 8, 128), F32),
            pltpu.VMEM((4, 8, 8, 128), F32),
            pltpu.VMEM((8, 8, 128), F32),
            pltpu.VMEM((8, 8, 128), F32),
            pltpu.VMEM((4, 8, 128), F32),
            pltpu.VMEM((2, 8, 128), F32),
            pltpu.VMEM((8, 4, 8, 128), F32),
            pltpu.VMEM((2, 256, 128), F32),
            pltpu.VMEM((16, 2, 4, 128), F32),
            pltpu.VMEM((16, 2, 4, 128), F32),
            dma((9,)), dma((8,)), dma((8,)),
            dma((2, 7)), dma((2, 7)), dma((8,)), dma((8,)), dma((3,)), dma((3,)),
            dma((1,)), dma((1,)), dma((4,)), dma((4,)), dma((8,)), dma((8,)),
            dma((4,)), dma((4,)), dma((1,)), dma((1,)),
            dma((4,)), dma((4,)), dma((8,)), dma((8,)), dma((16,)), dma((16,)),
        ],
        compiler_params=pltpu.CompilerParams(collective_id=0, has_side_effects=True, vmem_limit_bytes=40 << 20),
        cost_estimate=pl.CostEstimate(flops=20 << 20, bytes_accessed=6 << 20, transcendentals=0),
        name="reduce_and_smooth",
    )(parts, pooled, smooth_age, smooth_dur, credibility)


def per_device(
    age_cell, dur_cell, trans_code, age_frac, dur_frac, exposure, claims, block_tile, smooth_age, smooth_dur, credibility
):
    fields = [
        f.reshape(-1, 128) for f in (age_cell, dur_cell, trans_code, age_frac, dur_frac, exposure, claims)
    ]
    parts, pooled = grids(block_tile.reshape(-1), fields)
    return smooth(parts, pooled, smooth_age, smooth_dur, credibility)


def solution(mesh):
    split = Mesh(mesh.devices.reshape(mesh.shape["tg"], 8, 4, 2), ("tg", "z", "y", "c"))
    tile = ("z", "y", "c")
    placed = (P("tg", tile),) * 7 + (P("tg", tile, None),) + (P("tg"),) * 3
    return jax.shard_map(
        per_device,
        mesh=split,
        in_specs=placed,
        out_specs=(P("tg", tile, None),) * 2,
        check_vma=False,
    )
```

time: 96.9 us -> 85.1 us (0.88)
  Pallas kernels: 87.3 us -> 75.5 us
    pallas_call x1, Pallas kernels: 62.9 us -> 48.7 us  [smooth(): pl.pallas_call(smooth_kernel, out_shape=(jax.ShapeDtypeStruct((16, 4, 128...]
    pallas_call x1, Pallas kernels: 24.4 us -> 26.8 us  [grids(): pl.pallas_call(grid_kernel, out_shape=(jax.ShapeDtypeStruct((2, 32, 128,...]
where the time goes in v2:
time: 85.1 us; the launch traced here: 84.7 us
  Pallas kernels  75.5 us (89%)
  local copies, waits for them, and re-layouts  8.56 us (10%)
    pallas_call x1, Pallas kernels, smooth(): pl.pallas_call(smooth_kernel, out_shape=(jax.ShapeDtypeStruct((16, 4, 128...  48.7 us
    pallas_call x1, Pallas kernels, grids(): pl.pallas_call(grid_kernel, out_shape=(jax.ShapeDtypeStruct((2, 32, 128,...  26.8 us
    unnamed x24, local copies, waits for them, and re-layouts  8.56 us

profile of v2, /device:TPU:1, one launch (start us, length us, event | category | flops | bytes accessed | tf_op | source)
XLA Modules:
  0.0 84.7 jit_solution(2054901202382199961)
XLA Ops:
  0.6 0.0 copy-start.3
  0.6 0.9 %copy-done.3 = s32[1,65536]{1,0:T(1,128)S(1)} copy-done((s32[1,65536]{1,0:T(1,128)S(1)}, s32[1,65536]{1,0:T(1,128)}, u32[]{:S(2)}) %copy-start.3) | copy-done | bytes 262168
  1.6 0.9 %copy-done.4 = s32[1,65536]{1,0:T(1,128)S(1)} copy-done((s32[1,65536]{1,0:T(1,128)S(1)}, s32[1,65536]{1,0:T(1,128)}, u32[]{:S(2)}) %copy-start.4) | copy-done | bytes 262168
  2.5 0.0 copy-start.5
  2.5 0.9 %copy-done.5 = s32[1,65536]{1,0:T(1,128)S(1)} copy-done((s32[1,65536]{1,0:T(1,128)S(1)}, s32[1,65536]{1,0:T(1,128)}, u32[]{:S(2)}) %copy-start.5) | copy-done | bytes 262168
  3.5 0.0 copy-start.6
  3.5 0.9 %copy-done.6 = f32[1,65536]{1,0:T(1,128)S(1)} copy-done((f32[1,65536]{1,0:T(1,128)S(1)}, f32[1,65536]{1,0:T(1,128)}, u32[]{:S(2)}) %copy-start.6) | copy-done | bytes 262168
  4.4 0.0 copy-start.7
  4.4 0.9 %copy-done.7 = f32[1,65536]{1,0:T(1,128)S(1)} copy-done((f32[1,65536]{1,0:T(1,128)S(1)}, f32[1,65536]{1,0:T(1,128)}, u32[]{:S(2)}) %copy-start.7) | copy-done | bytes 262168
  5.4 0.0 copy-start.8
  5.4 0.9 %copy-done.8 = f32[1,65536]{1,0:T(1,128)S(1)} copy-done((f32[1,65536]{1,0:T(1,128)S(1)}, f32[1,65536]{1,0:T(1,128)}, u32[]{:S(2)}) %copy-start.8) | copy-done | bytes 262168
  6.3 0.0 copy-start.9
  6.3 0.9 %copy-done.9 = f32[1,65536]{1,0:T(1,128)S(1)} copy-done((f32[1,65536]{1,0:T(1,128)S(1)}, f32[1,65536]{1,0:T(1,128)}, u32[]{:S(2)}) %copy-start.9) | copy-done | bytes 262168
  7.3 0.0 copy-start.10
  7.3 0.7 copy-done.10
  8.0 0.0 copy-start
  8.0 0.0 copy-start.1
  8.0 26.8 %local_grid.1 = (f32[2,32,128,128]{3,2,1,0:T(8,128)S(1)}, f32[2,32,8,128]{3,2,1,0:T(8,128)S(1)}) custom-call(s32[512]{0:T(512)S(1)} %bitcast.15, s32[512,128]{1,0:T(8,128)S(1)} %bitcast.8, s32[512,128]{1,0:T(8,128)S(1)} %bitcast.9, s32[512,128]{1,0:T(8,128)S(1)} %bitcast.10, f32[512,128]{1,0:T(8,128)S(1)} %bitcast.11, f32[512,128]{1,0:T(8,128)S(1)} %bitcast.12, ...), custom_call_target="tpu_custom_call" | custom-call | flops 4294967296 | bytes 6291456 | tf_op jit(solution)/shard_map/local_grid/pallas_call | solution.py:121
  34.7 0.0 copy-done
  34.7 0.0 copy-done.1
  34.8 0.0 copy-done.2
  34.8 48.7 %reduce_and_smooth.1 = (f32[16,4,128]{2,1,0:T(4,128)S(1)}, f32[16,4,128]{2,1,0:T(4,128)S(1)}) custom-call(f32[2,32,128,128]{3,2,1,0:T(8,128)S(1)} %get-tuple-element.4.g_ref, f32[2,32,8,128]{3,2,1,0:T(8,128)S(1)} %get-tuple-element.5.p_ref, f32[16]{0:T(128)S(1)} %copy-done, f32[16]{0:T(128)S(1)} %copy-done.1, f32[16]{0:T(128)S(1)} %copy-done.2), custom_call_target="tpu_custom_call" | custom-call | flops 20971520 | bytes 6291456 | tf_op jit(solution)/shard_map/reduce_and_smooth/pallas_call | solution.py:432
  83.5 0.6 copy.15
  84.1 0.6 copy.16
  (2 shorter events, 0.0 us)
Async XLA Ops:
  0.6 1.0 %copy-start.3 = (s32[1,65536]{1,0:T(1,128)S(1)}, s32[1,65536]{1,0:T(1,128)}, u32[]{:S(2)}) copy-start(s32[1,65536]{1,0:T(1,128)} %param.11) | copy-start | bytes 786436
  1.6 0.9 %copy-start.4 = (s32[1,65536]{1,0:T(1,128)S(1)}, s32[1,65536]{1,0:T(1,128)}, u32[]{:S(2)}) copy-start(s32[1,65536]{1,0:T(1,128)} %param.12) | copy-start | bytes 786436
  2.5 0.9 %copy-start.5 = (s32[1,65536]{1,0:T(1,128)S(1)}, s32[1,65536]{1,0:T(1,128)}, u32[]{:S(2)}) copy-start(s32[1,65536]{1,0:T(1,128)} %param.13) | copy-start | bytes 786436
  3.5 0.9 %copy-start.6 = (f32[1,65536]{1,0:T(1,128)S(1)}, f32[1,65536]{1,0:T(1,128)}, u32[]{:S(2)}) copy-start(f32[1,65536]{1,0:T(1,128)} %param.14) | copy-start | bytes 786436
  4.4 0.9 %copy-start.7 = (f32[1,65536]{1,0:T(1,128)S(1)}, f32[1,65536]{1,0:T(1,128)}, u32[]{:S(2)}) copy-start(f32[1,65536]{1,0:T(1,128)} %param.15) | copy-start | bytes 786436
  5.4 0.9 %copy-start.8 = (f32[1,65536]{1,0:T(1,128)S(1)}, f32[1,65536]{1,0:T(1,128)}, u32[]{:S(2)}) copy-start(f32[1,65536]{1,0:T(1,128)} %param.16) | copy-start | bytes 786436
  6.3 0.9 %copy-start.9 = (f32[1,65536]{1,0:T(1,128)S(1)}, f32[1,65536]{1,0:T(1,128)}, u32[]{:S(2)}) copy-start(f32[1,65536]{1,0:T(1,128)} %param.17) | copy-start | bytes 786436
  7.3 0.7 copy-start.10
  8.0 26.8 %copy-start = (f32[16]{0:T(128)S(1)}, f32[16]{0:T(128)}, u32[]{:S(2)}) copy-start(f32[16]{0:T(128)} %age_weight.1) | copy-start | bytes 196
  8.0 26.8 %copy-start.1 = (f32[16]{0:T(128)S(1)}, f32[16]{0:T(128)}, u32[]{:S(2)}) copy-start(f32[16]{0:T(128)} %dur_weight.1) | copy-start | bytes 196
  8.0 26.8 %copy-start.2 = (f32[16]{0:T(128)S(1)}, f32[16]{0:T(128)}, u32[]{:S(2)}) copy-start(f32[16]{0:T(128)} %credibility.1) | copy-start | bytes 196

commit v3 on v2

--- a/solution.py
+++ b/solution.py
@@ -18,18 +18,21 @@
     return (r * r * r * s, (3.0 * c - 6.0 * f2 + 4.0) * s, (-3.0 * c + 3.0 * f2 + 3.0 * f + 1.0) * s, c * s)
 
 def grid_kernel(
-    tile_ref, age_hbm, dur_hbm, code_hbm, af_hbm, df_hbm, ex_hbm, cl_hbm, out_ref, pool_ref,
-    acc, age_ref, dur_ref, code_ref, af_ref, df_ref, ex_ref, cl_ref, sem,
+    tile_ref, age_hbm, dur_hbm, code_hbm, af_hbm, df_hbm, ex_hbm, cl_hbm, out_hbm, pool_hbm,
+    acc, age_ref, dur_ref, code_ref, af_ref, df_ref, ex_ref, cl_ref, weights, out_ref, pool_ref, sem, out_sem,
 ):
-    loads = []
+    pairs = (
+        (age_hbm, age_ref), (dur_hbm, dur_ref), (code_hbm, code_ref), (af_hbm, af_ref),
+        (df_hbm, df_ref), (ex_hbm, ex_ref), (cl_hbm, cl_ref),
+    )
+
+    def loads(part):
+        at = pl.ds(part * 128, 128)
+        return [pltpu.make_async_copy(src.at[at], dst.at[at], sem.at[part, k]) for k, (src, dst) in enumerate(pairs)]
+
     for part in range(4):
-        at = pl.ds(part * 128, 128)
-        for k, (src, dst) in enumerate((
-            (age_hbm, age_ref), (dur_hbm, dur_ref), (code_hbm, code_ref), (af_hbm, af_ref),
-            (df_hbm, df_ref), (ex_hbm, ex_ref), (cl_hbm, cl_ref),
-        )):
-            loads.append(pltpu.make_async_copy(src.at[at], dst.at[at], sem.at[part, k]))
-            loads[-1].start()
+        for load in loads(part):
+            load.start()
     acc[...] = jnp.zeros(acc.shape, F32)
     iota8 = lax.broadcasted_iota(I32, (8, 128), 0)
     iota16 = lax.broadcasted_iota(I32, (16, 128), 0)
@@ -37,100 +40,129 @@
     zero16 = jnp.zeros((16, 128), BF16)
     r1 = iota16 + 1
 
-    def group(g, _):
+    def twice(v):
+        return jnp.concatenate([v, v], 0)
+
+    def group(g, slot):
         base = pl.multiple_of(g * 8, 8)
         at = pl.ds(base, 8)
-        aw = spline(af_ref[at, :])
-        dw = spline(df_ref[at, :])
-        age, dc = age_ref[at, :], dur_ref[at, :]
-        code = code_ref[at, :].astype(F32)
-        ex, cl = ex_ref[at, :], cl_ref[at, :]
+        for k, v in enumerate(spline(af_ref[at, :]) + spline(df_ref[at, :])):
+            weights[slot, k] = v
         for i in range(8):
-            def row(x, n):
-                return jnp.broadcast_to(x[i : i + 1, :], (n, 128))
-            delta = iota8 - row(dc, 8)
-            w = jnp.where(delta == 0, row(dw[0], 8), 0.0)
+            def row(ref):
+                return ref[pl.ds(base + i, 8, stride=0), :]
+
+            def weight(k):
+                return weights[slot, k, pl.ds(i, 8, stride=0), :]
+
+            delta = iota8 - row(dur_ref)
+            w = jnp.where(delta == 0, weight(4), 0.0)
             for k in range(1, 4):
-                w = jnp.where(delta == k, row(dw[k], 8), w)
-            e = w * row(ex, 8)
-            c = w * row(cl, 8)
-            e16 = jnp.concatenate([e, e], 0).astype(BF16)
-            c16 = jnp.concatenate([c, c], 0).astype(BF16)
-            code16 = row(code, 16).astype(BF16)
-            le, lc = [], []
-            rel = code16 - half16
+                w = jnp.where(delta == k, weight(4 + k), w)
+            e16 = twice(w * row(ex_ref)).astype(BF16)
+            c16 = twice(w * row(cl_ref)).astype(BF16)
+            code = twice(row(code_ref)).astype(F32).astype(BF16) - half16
+            left_e, left_c = [], []
             for j in range(8):
-                m = rel == jnp.bfloat16(2 * j)
-                le.append(jnp.where(m, e16, zero16))
-                lc.append(jnp.where(m, c16, zero16))
-            lhs = jnp.concatenate(le + lc, 0)
-            ageb = row(age, 16)
-            kk = (r1 - ageb) & 15
-            a = jnp.where(kk == 0, row(aw[0], 16), 0.0)
+                m = code == jnp.bfloat16(2 * j)
+                left_e.append(jnp.where(m, e16, zero16))
+                left_c.append(jnp.where(m, c16, zero16))
+            left = jnp.concatenate(left_e + left_c, 0)
+            age = twice(row(age_ref))
+            kk = (r1 - age) & 15
+            a = jnp.where(kk == 0, twice(weight(0)), 0.0)
             for k in range(1, 4):
-                a = jnp.where(kk == k, row(aw[k], 16), a)
+                a = jnp.where(kk == k, twice(weight(k)), a)
             a16 = a.astype(BF16)
-            grp = ((ageb - 1 + kk) >> 4).astype(F32).astype(BF16)
-            rhs = jnp.concatenate([jnp.where(grp == jnp.bfloat16(q), a16, zero16) for q in range(8)], 0)
-            res = lax.dot_general(lhs, rhs, (((1,), (1,)), ((), ())), preferred_element_type=F32)
+            block = ((age - 1 + kk) >> 4).astype(F32).astype(BF16)
+            right = jnp.concatenate([jnp.where(block == jnp.bfloat16(q), a16, zero16) for q in range(8)], 0)
+            res = lax.dot_general(left, right, (((1,), (1,)), ((), ())), preferred_element_type=F32)
             tile = tile_ref[g * 8 + i]
-            idx = (tile & 1) * 32 + (tile >> 1)
-            acc[idx] += res
-        return 0
-
-    for part in range(4):
-        for load in loads[part * 7 : part * 7 + 7]:
+            acc[(tile & 1) * 32 + (tile >> 1)] += res
+
+    def groups(step, carry):
+        for slot in range(8):
+            group(step * 8 + slot, slot)
+        return carry
+
+    def quarter(part, carry):
+        for load in loads(part):
             load.wait()
-        lax.fori_loop(part * 16, part * 16 + 16, group, 0)
-
-    sub = lax.broadcasted_iota(I32, (8, 128), 0)
-
-    def comb(m, _):
-        h = m // 16
-        s = (m % 16) // 8
-        r8 = pl.multiple_of((m % 8) * 8, 8)
+        return lax.fori_loop(part * 2, part * 2 + 2, groups, carry)
+
+    lax.fori_loop(0, 4, quarter, 0)
+
+    low = iota8 < 4
+    stores = []
+
+    def joined(m, h, s):
+        r8 = pl.multiple_of(lax.rem(m, 8) * 8, 8)
         up = jnp.minimum(m + 1, 31)
         dn = jnp.maximum(m - 1, 0)
-        pooled = [jnp.zeros((8, 128), F32), jnp.zeros((8, 128), F32)]
+        end = (iota8 == 0) & (m == 31)
+        begin = (iota8 >= 5) & (m == 0)
+        pooled = []
         for ch in range(2):
+            total = jnp.zeros((8, 128), F32)
             for t in range(16):
-                ct = ch * 16 + t
-                sl = pl.ds(ct * 8, 8)
-                ev = jnp.where(sub == 0, acc[up, sl, :], acc[m, sl, :])
-                ev = jnp.where((sub == 0) & (m == 31), 0.0, ev)
-                ev = pltpu.roll(ev, 7, 0)
-                od = jnp.where(sub >= 5, acc[32 + dn, sl, :], acc[32 + m, sl, :])
-                od = jnp.where((sub >= 5) & (m == 0), 0.0, od)
-                od = pltpu.roll(od, 3, 0)
-                v = ev + od
-                pooled[ch] = pooled[ch] + v
+                sl = pl.ds((ch * 16 + t) * 8, 8)
+                ev = jnp.where(iota8 == 0, acc[up, sl, :], acc[m, sl, :])
+                ev = pltpu.roll(jnp.where(end, 0.0, ev), 7, 0)
+                od = jnp.where(iota8 >= 5, acc[32 + dn, sl, :], acc[32 + m, sl, :])
+                v = ev + pltpu.roll(jnp.where(begin, 0.0, od), 3, 0)
+                total = total + v
                 z, y = t >> 1, 2 * (t & 1) + s
-                slot = jnp.where(h == 0, y * 8 + z, z * 4 + y)
-                out_ref[h, slot, pl.ds(ch * 64 + r8, 8), :] = v
+                out_ref[h, y * 8 + z if h == 0 else z * 4 + y, pl.ds(ch * 64 + r8, 8), :] = v
+            pooled.append(total)
         pe, po = pooled
-        low = sub < 4
-        z, y = m // 4, m % 4
-        pool_ref[0, y * 8 + z] = jnp.where(low, pe, pltpu.roll(po, 4, 0))
-        pool_ref[1, y * 8 + z] = jnp.where(low, pltpu.roll(pe, 4, 0), po)
-        return 0
-
-    lax.fori_loop(0, 32, comb, 0)
+        at = lax.rem(m, 4) * 8 + m // 4
+        pool_ref[0, at] = jnp.where(low, pe, pltpu.roll(po, 4, 0))
+        pool_ref[1, at] = jnp.where(low, pltpu.roll(pe, 4, 0), po)
+
+    for h in range(2):
+        for s in range(2):
+            first = h * 16 + s * 8
+
+            def some(step, carry):
+                for k in range(4):
+                    joined(first + step * 4 + k, h, s)
+                return carry
+
+            lax.fori_loop(0, 2, some, 0)
+            if h == 0:
+                slots = [pl.ds(y * 8, 8) for y in (s, s + 2)]
+            else:
+                slots = [z * 4 + y for z in range(8) for y in (s, s + 2)]
+            for k, at in enumerate(slots):
+                stores.append(pltpu.make_async_copy(out_ref.at[h, at], out_hbm.at[h, at], out_sem.at[h * 2 + s, k]))
+                stores[-1].start()
+    stores.append(pltpu.make_async_copy(pool_ref, pool_hbm, out_sem.at[4, 0]))
+    stores[-1].start()
+    for store in stores:
+        store.wait()
+
 
 def grids(tiles, fields):
-    vmem = pl.BlockSpec(memory_space=pltpu.VMEM)
+    whole = pl.BlockSpec(memory_space=HBM)
     return pl.pallas_call(
         grid_kernel,
         out_shape=(
             jax.ShapeDtypeStruct((2, 32, 128, 128), F32),
             jax.ShapeDtypeStruct((2, 32, 8, 128), F32),
         ),
-        in_specs=[pl.BlockSpec(memory_space=pltpu.SMEM)] + [pl.BlockSpec(memory_space=HBM)] * 7,
-        out_specs=(vmem, vmem),
+        in_specs=[pl.BlockSpec(memory_space=pltpu.SMEM)] + [whole] * 7,
+        out_specs=(whole, whole),
         scratch_shapes=[pltpu.VMEM((64, 256, 128), F32)]
         + [pltpu.VMEM((512, 128), I32)] * 3
         + [pltpu.VMEM((512, 128), F32)] * 4
-        + [pltpu.SemaphoreType.DMA((4, 7))],
-        compiler_params=pltpu.CompilerParams(vmem_limit_bytes=40 << 20),
+        + [
+            pltpu.VMEM((8, 8, 8, 128), F32),
+            pltpu.VMEM((2, 32, 128, 128), F32),
+            pltpu.VMEM((2, 32, 8, 128), F32),
+            pltpu.SemaphoreType.DMA((4, 7)),
+            pltpu.SemaphoreType.DMA((5, 16)),
+        ],
+        compiler_params=pltpu.CompilerParams(vmem_limit_bytes=63 << 20),
         cost_estimate=pl.CostEstimate(flops=2 * 512 * 256 * 128 * 128, bytes_accessed=6 << 20, transcendentals=0),
         name="local_grid",
     )(tiles, *fields)
@@ -457,7 +489,7 @@
             dma((4,)), dma((4,)), dma((1,)), dma((1,)),
             dma((4,)), dma((4,)), dma((8,)), dma((8,)), dma((16,)), dma((16,)),
         ],
-        compiler_params=pltpu.CompilerParams(collective_id=0, has_side_effects=True, vmem_limit_bytes=40 << 20),
+        compiler_params=pltpu.CompilerParams(collective_id=0, has_side_effects=True, vmem_limit_bytes=63 << 20),
         cost_estimate=pl.CostEstimate(flops=20 << 20, bytes_accessed=6 << 20, transcendentals=0),
         name="reduce_and_smooth",
     )(parts, pooled, smooth_age, smooth_dur, credibility)

time: 85.1 us -> 71.8 us (0.84)
  Pallas kernels: 75.5 us -> 68.1 us
  local copies, waits for them, and re-layouts: 8.56 us -> 2.75 us
    pallas_call x1, Pallas kernels: 26.8 us -> 17.7 us  [grids(): pl.pallas_call(grid_kernel, out_shape=(jax.ShapeDtypeStruct((2, 32, 128,...]
    unnamed x24 -> x2, local copies, waits for them, and re-layouts: 8.56 us -> 2.75 us
    pallas_call x1, Pallas kernels: 48.7 us -> 50.3 us  [smooth(): pl.pallas_call(smooth_kernel, out_shape=(jax.ShapeDtypeStruct((16, 4, 128...]
where the time goes in v3:
time: 71.8 us; the launch traced here: 71.5 us
  Pallas kernels  68.1 us (95%)
  local copies, waits for them, and re-layouts  2.75 us (4%)
    pallas_call x1, Pallas kernels, smooth(): pl.pallas_call(smooth_kernel, out_shape=(jax.ShapeDtypeStruct((16, 4, 128...  50.3 us
    pallas_call x1, Pallas kernels, grids(): pl.pallas_call(grid_kernel, out_shape=(jax.ShapeDtypeStruct((2, 32, 128,...  17.7 us
    unnamed x2, local copies, waits for them, and re-layouts  2.75 us

profile of v3, /device:TPU:1, one launch (start us, length us, event | category | flops | bytes accessed | tf_op | source)
XLA Modules:
  0.0 71.5 jit_solution(1293946826431939180)
XLA Ops:
  0.6 17.7 %local_grid.1 = (f32[2,32,128,128]{3,2,1,0:T(8,128)}, f32[2,32,8,128]{3,2,1,0:T(8,128)}) custom-call(s32[512]{0:T(512)} %bitcast.15, s32[512,128]{1,0:T(8,128)} %bitcast.8, s32[512,128]{1,0:T(8,128)} %bitcast.9, s32[512,128]{1,0:T(8,128)} %bitcast.10, f32[512,128]{1,0:T(8,128)} %bitcast.11, f32[512,128]{1,0:T(8,128)} %bitcast.12, f32[512,128]{1,0:T(8,128)} %bitcast.13, ...), custom_call_target="tpu_custom_call" | custom-call | flops 4294967296 | bytes 6291456 | tf_op jit(solution)/shard_map/local_grid/pallas_call | solution.py:147
  18.4 50.3 %reduce_and_smooth.1 = (f32[16,4,128]{2,1,0:T(4,128)}, f32[16,4,128]{2,1,0:T(4,128)}) custom-call(f32[2,32,128,128]{3,2,1,0:T(8,128)} %get-tuple-element.4.g_ref, f32[2,32,8,128]{3,2,1,0:T(8,128)} %get-tuple-element.5.p_ref, f32[16]{0:T(128)} %age_weight.1, f32[16]{0:T(128)} %dur_weight.1, f32[16]{0:T(128)} %credibility.1), custom_call_target="tpu_custom_call" | custom-call | flops 20971520 | bytes 6291456 | tf_op jit(solution)/shard_map/reduce_and_smooth/pallas_call | solution.py:464
  68.7 1.4 %copy.15 = f32[16,4,128]{2,1,0:T(4,128)} copy(f32[16,4,128]{2,1,0:T(4,128)} %get-tuple-element.8) | data formatting | bytes 65536
  70.1 1.4 %copy.16 = f32[16,4,128]{2,1,0:T(4,128)} copy(f32[16,4,128]{2,1,0:T(4,128)} %get-tuple-element.9) | data formatting | bytes 65536

commit v4 on v3

--- a/solution.py
+++ b/solution.py
@@ -226,10 +226,9 @@
 
 def smooth_kernel(
     g_ref, p_ref, age_weight, dur_weight, credibility, out_s, out_r,
-    part, other, land1, land2, grid, pool_in, pool_part, pool_y, pool_z, pool_zin, pool, twin, prior, field, done, got,
+    part, other, land1, land2, grid, pool_y, pool_z, pool_zin, pool, prior, field, done, got,
     local_sem, s0_send, s0_recv, s1_send, s1_recv, s2_send, s2_recv, ag_send, ag_recv,
-    pa_send, pa_recv, pb_send, pb_recv, pc_send, pc_recv, x_send, x_recv, t_send, t_recv,
-    y_send, y_recv, z_send, z_recv, o_send, o_recv,
+    pb_send, pb_recv, pc_send, pc_recv, x_send, x_recv, y_send, y_recv, z_send, z_recv, o_send, o_recv,
 ):
     x, z, y, c = (lax.axis_index(a) for a in ("tg", "z", "y", "c"))
     sibling = (x, z, y, 1 - c)
@@ -242,12 +241,10 @@
     def along_z(d):
         return (x, lax.rem(z + d, 8), y, c)
 
-    def along_x(d):
-        return (lax.rem(x + d, 4), z, y, c)
-
     barrier = pltpu.get_barrier_semaphore()
-    peers = [sibling, (x, z, pair, 1 - c)]
-    peers += [along_y(d) for d in range(1, 4)] + [along_z(d) for d in range(1, 8)] + [along_x(d) for d in range(1, 4)]
+    peers = [sibling] + [along_z(d) for d in range(1, 8)]
+    for e in (c, 1 - c):
+        peers += [(x, z, lax.rem(y + d, 4), e) for d in range(1, 4)] + [(lax.rem(x + d, 4), z, y, e) for d in range(1, 4)]
     for peer in peers:
         pl.semaphore_signal(barrier, inc=1, device_id=peer, device_id_type=MESH)
     pl.semaphore_wait(barrier, len(peers))
@@ -275,59 +272,51 @@
             move.start()
             sends.append(move)
 
-        def pool_to_sibling():
-            send(p_ref.at[1 - core], pool_in, pa_send.at[0], pa_recv.at[0], sibling)
-            own = pltpu.make_async_copy(p_ref.at[core], pool_part, local_sem.at[8])
+        def pool_along_y():
+            own = pltpu.make_async_copy(p_ref.at[core, pl.ds(y * 8, 8)], pool_y.at[0], local_sem.at[8])
             own.start()
+            for k in (4, 5, 2, 3, 6, 7, 1):
+                d, e = k // 2, k % 2
+                to, yy = core ^ e, lax.rem(y + d, 4)
+                send(p_ref.at[to, pl.ds(yy * 8, 8)], pool_y.at[k], pb_send.at[k], pb_recv.at[k], (x, z, yy, to))
             return own
 
-        def pool_along_y():
+        def pool_along_z():
             pool_own.wait()
-            arrive(pool_in, pa_recv.at[0])
-            pool_part[...] += pool_in[...]
-            for d in (2, 1, 3):
-                at = pl.ds(lax.rem(y + d, 4) * 8, 8)
-                send(pool_part.at[at], pool_y.at[d], pb_send.at[d], pb_recv.at[d], along_y(d))
-
-        def pool_along_z():
-            for d in range(1, 4):
-                arrive(pool_y.at[d], pb_recv.at[d])
-            pool_z[...] = (pool_part[pl.ds(y * 8, 8)] + pool_y[1]) + (pool_y[2] + pool_y[3])
+            total = pool_y[0]
+            for k in range(1, 8):
+                arrive(pool_y.at[k], pb_recv.at[k])
+                total = total + pool_y[k]
+            pool_z[...] = total
             for d in (4, 3, 5, 2, 6, 1, 7):
                 send(pool_z.at[lax.rem(z + d, 8)], pool_zin.at[d], pc_send.at[d], pc_recv.at[d], along_z(d))
 
         def pool_along_x():
+            total = pool_z[z]
             for d in range(1, 8):
                 arrive(pool_zin.at[d], pc_recv.at[d])
-            total = pool_z[z]
-            for d in range(1, 8):
                 total = total + pool_zin[d]
             pool[0] = total
             for d in (2, 1, 3):
-                send(pool.at[0], pool.at[d], x_send.at[d], x_recv.at[d], along_x(d))
-
-        def prior_to_sibling():
+                send(pool.at[0], pool.at[d], x_send.at[d], x_recv.at[d], (lax.rem(x + d, 4), z, y, core))
+
+        def prior_along_z():
             for d in range(1, 4):
                 arrive(pool.at[d], x_recv.at[d])
             total = (pool[0] + pool[1]) + (pool[2] + pool[3])
-            twin[0] = pltpu.roll(total, 4, 0) / (1.0 + total)
-            send(twin.at[0], twin.at[1], t_send.at[0], t_recv.at[0], sibling)
+            prior[y * 2 + core, z] = pltpu.roll(total, 4, 0) / (1.0 + total)
+            for d in (4, 3, 5, 2, 6, 1, 7):
+                at = prior.at[y * 2 + core, z]
+                send(at, at, z_send.at[d], z_recv.at[d], along_z(d))
 
         def prior_along_y():
-            arrive(twin.at[1], t_recv.at[0])
-            low, high = twin[core], twin[1 - core]
-            under = lax.broadcasted_iota(I32, (8, 128), 0) < 4
-            prior[z, y] = jnp.where(under, low, pltpu.roll(high, 4, 0))
-            for d in (2, 1, 3):
-                send(prior.at[z, y], prior.at[z, y], y_send.at[d], y_recv.at[d], along_y(d))
-
-        def prior_along_z():
-            for d in range(1, 4):
-                arrive(prior.at[z, lax.rem(y + 4 - d, 4)], y_recv.at[d])
-            for d in (4, 3, 5, 2, 6, 1, 7):
-                send(prior.at[z], prior.at[z], z_send.at[d], z_recv.at[d], along_z(d))
-
-        pool_own = pool_to_sibling()
+            for d in range(1, 8):
+                arrive(prior.at[y * 2 + core, lax.rem(z + 8 - d, 8)], z_recv.at[d])
+            for k in (4, 5, 2, 3, 6, 7, 1):
+                at = prior.at[y * 2 + core]
+                send(at, at, y_send.at[k], y_recv.at[k], (x, z, lax.rem(y + k // 2, 4), core ^ (k % 2)))
+
+        pool_own = pool_along_y()
         sib_n, sib_i = (8, z) if core == 0 else (4, y)
         sib_many = 32 // sib_n
         for j, d in enumerate(dests(sib_n, sib_i)):
@@ -359,9 +348,8 @@
 
         def hook(j):
             if j in points:
-                points[j](pool_along_z, pool_along_x, prior_to_sibling)
-
-        pool_along_y()
+                points[j](pool_along_z, pool_along_x, prior_along_z)
+
         sends += reduce_along(n, i, first_axis, piece, land, s1_send, s1_recv, prepare, hook)
 
         far = sorted(range(1, n2), key=lambda d: -min(d, n2 - d))
@@ -375,9 +363,8 @@
             grid[quarter] += land2[d]
         for j, peer in enumerate((sibling, (x, z, pair, c), (x, z, pair, 1 - c))):
             send(grid.at[quarter], grid.at[quarter], ag_send.at[j], ag_recv.at[j], peer)
-        prior_along_z()
-        for d in range(1, 8):
-            arrive(prior.at[lax.rem(z + 8 - d, 8)], z_recv.at[d])
+        for k in range(1, 8):
+            arrive(prior.at[lax.rem(y + 4 - k // 2, 4) * 2 + (core ^ (k % 2))], y_recv.at[k])
         for j, q in enumerate((2 * (1 - core) + side, 2 * core + 1 - side, 2 * (1 - core) + 1 - side)):
             arrive(grid.at[q], ag_recv.at[j])
         for move in sends:
@@ -400,7 +387,11 @@
     expo = jnp.concatenate([grid[q, 0:64] for q in range(4)], 0)
     claim = jnp.concatenate([grid[q, 64:128] for q in range(4)], 0)
     diagonal = expo + cred
-    residual = claim + cred * prior[...].reshape(256, 128)
+    under = lax.broadcasted_iota(I32, (8, 128), 0) < 4
+    pooled = [
+        jnp.where(under, prior[2 * yy, zz], pltpu.roll(prior[2 * yy + 1, zz], 4, 0)) for zz in range(8) for yy in range(4)
+    ]
+    residual = claim + cred * jnp.concatenate(pooled, 0)
     direction = residual
     smoothed = jnp.zeros_like(residual)
 
@@ -472,24 +463,20 @@
             pltpu.VMEM((28, 128, 128), F32),
             pltpu.VMEM((8, 128, 128), F32),
             pltpu.VMEM((4, 128, 128), F32),
-            pltpu.VMEM((32, 8, 128), F32),
-            pltpu.VMEM((32, 8, 128), F32),
-            pltpu.VMEM((4, 8, 8, 128), F32),
+            pltpu.VMEM((8, 8, 8, 128), F32),
             pltpu.VMEM((8, 8, 128), F32),
             pltpu.VMEM((8, 8, 128), F32),
-            pltpu.VMEM((4, 8, 128), F32),
-            pltpu.VMEM((2, 8, 128), F32),
-            pltpu.VMEM((8, 4, 8, 128), F32),
+            pltpu.VMEM((8, 8, 128), F32),
+            pltpu.VMEM((8, 8, 8, 128), F32),
             pltpu.VMEM((2, 256, 128), F32),
             pltpu.VMEM((16, 2, 4, 128), F32),
             pltpu.VMEM((16, 2, 4, 128), F32),
             dma((9,)), dma((8,)), dma((8,)),
             dma((2, 7)), dma((2, 7)), dma((8,)), dma((8,)), dma((3,)), dma((3,)),
-            dma((1,)), dma((1,)), dma((4,)), dma((4,)), dma((8,)), dma((8,)),
-            dma((4,)), dma((4,)), dma((1,)), dma((1,)),
-            dma((4,)), dma((4,)), dma((8,)), dma((8,)), dma((16,)), dma((16,)),
+            dma((8,)), dma((8,)), dma((8,)), dma((8,)), dma((8,)), dma((8,)),
+            dma((8,)), dma((8,)), dma((8,)), dma((8,)), dma((16,)), dma((16,)),
         ],
-        compiler_params=pltpu.CompilerParams(collective_id=0, has_side_effects=True, vmem_limit_bytes=63 << 20),
+        compiler_params=pltpu.CompilerParams(collective_id=0, has_side_effects=True, vmem_limit_bytes=(64 << 20) - (200 << 10)),
         cost_estimate=pl.CostEstimate(flops=20 << 20, bytes_accessed=6 << 20, transcendentals=0),
         name="reduce_and_smooth",
     )(parts, pooled, smooth_age, smooth_dur, credibility)

time: 71.8 us -> 70.7 us (0.985)
  Pallas kernels: 68.1 us -> 67 us
    pallas_call x1, Pallas kernels: 50.3 us -> 49.2 us  [smooth(): pl.pallas_call(smooth_kernel, out_shape=(jax.ShapeDtypeStruct((16, 4, 128...]
where the time goes in v4:
time: 70.7 us; the launch traced here: 70.4 us
  Pallas kernels  67 us (95%)
  local copies, waits for them, and re-layouts  2.75 us (4%)
    pallas_call x1, Pallas kernels, smooth(): pl.pallas_call(smooth_kernel, out_shape=(jax.ShapeDtypeStruct((16, 4, 128...  49.2 us
    pallas_call x1, Pallas kernels, grids(): pl.pallas_call(grid_kernel, out_shape=(jax.ShapeDtypeStruct((2, 32, 128,...  17.7 us
    unnamed x2, local copies, waits for them, and re-layouts  2.75 us

profile of v4, /device:TPU:1, one launch (start us, length us, event | category | flops | bytes accessed | tf_op | source)
XLA Modules:
  0.0 70.4 jit_solution(6729902259577362316)
XLA Ops:
  0.6 17.7 %local_grid.1 = (f32[2,32,128,128]{3,2,1,0:T(8,128)}, f32[2,32,8,128]{3,2,1,0:T(8,128)}) custom-call(s32[512]{0:T(512)} %bitcast.15, s32[512,128]{1,0:T(8,128)} %bitcast.8, s32[512,128]{1,0:T(8,128)} %bitcast.9, s32[512,128]{1,0:T(8,128)} %bitcast.10, f32[512,128]{1,0:T(8,128)} %bitcast.11, f32[512,128]{1,0:T(8,128)} %bitcast.12, f32[512,128]{1,0:T(8,128)} %bitcast.13, ...), custom_call_target="tpu_custom_call" | custom-call | flops 4294967296 | bytes 6291456 | tf_op jit(solution)/shard_map/local_grid/pallas_call | solution.py:147
  18.4 49.2 %reduce_and_smooth.1 = (f32[16,4,128]{2,1,0:T(4,128)}, f32[16,4,128]{2,1,0:T(4,128)}) custom-call(f32[2,32,128,128]{3,2,1,0:T(8,128)} %get-tuple-element.4.g_ref, f32[2,32,8,128]{3,2,1,0:T(8,128)} %get-tuple-element.5.p_ref, f32[16]{0:T(128)} %age_weight.1, f32[16]{0:T(128)} %dur_weight.1, f32[16]{0:T(128)} %credibility.1), custom_call_target="tpu_custom_call" | custom-call | flops 20971520 | bytes 6291456 | tf_op jit(solution)/shard_map/reduce_and_smooth/pallas_call | solution.py:455
  67.6 1.4 %copy.15 = f32[16,4,128]{2,1,0:T(4,128)} copy(f32[16,4,128]{2,1,0:T(4,128)} %get-tuple-element.8) | data formatting | bytes 65536
  69.0 1.4 %copy.16 = f32[16,4,128]{2,1,0:T(4,128)} copy(f32[16,4,128]{2,1,0:T(4,128)} %get-tuple-element.9) | data formatting | bytes 65536

commit v5 on v4

--- a/solution.py
+++ b/solution.py
@@ -352,10 +352,10 @@
 
         sends += reduce_along(n, i, first_axis, piece, land, s1_send, s1_recv, prepare, hook)
 
+        prior_along_y()
         far = sorted(range(1, n2), key=lambda d: -min(d, n2 - d))
         for d in far:
             send(part.at[i * many + lax.rem(i2 + d, n2)], land2.at[d], s2_send.at[d], s2_recv.at[d], second_axis(d))
-        prior_along_y()
         quarter = 2 * core + side
         grid[quarter] = part[i * many + i2]
         for d in reversed(far):

time: 70.7 us -> 72.3 us (1.023)
  Pallas kernels: 67 us -> 68.6 us
    pallas_call x1, Pallas kernels: 49.2 us -> 50.9 us  [smooth(): pl.pallas_call(smooth_kernel, out_shape=(jax.ShapeDtypeStruct((16, 4, 128...]
where the time goes in v5:
time: 72.3 us; the launch traced here: 72 us
  Pallas kernels  68.6 us (95%)
  local copies, waits for them, and re-layouts  2.75 us (4%)
    pallas_call x1, Pallas kernels, smooth(): pl.pallas_call(smooth_kernel, out_shape=(jax.ShapeDtypeStruct((16, 4, 128...  50.9 us
    pallas_call x1, Pallas kernels, grids(): pl.pallas_call(grid_kernel, out_shape=(jax.ShapeDtypeStruct((2, 32, 128,...  17.7 us
    unnamed x2, local copies, waits for them, and re-layouts  2.75 us

profile of v5, /device:TPU:1, one launch (start us, length us, event | category | flops | bytes accessed | tf_op | source)
XLA Modules:
  0.0 72.0 jit_solution(14698169602388661911)
XLA Ops:
  0.6 17.7 %local_grid.1 = (f32[2,32,128,128]{3,2,1,0:T(8,128)}, f32[2,32,8,128]{3,2,1,0:T(8,128)}) custom-call(s32[512]{0:T(512)} %bitcast.15, s32[512,128]{1,0:T(8,128)} %bitcast.8, s32[512,128]{1,0:T(8,128)} %bitcast.9, s32[512,128]{1,0:T(8,128)} %bitcast.10, f32[512,128]{1,0:T(8,128)} %bitcast.11, f32[512,128]{1,0:T(8,128)} %bitcast.12, f32[512,128]{1,0:T(8,128)} %bitcast.13, ...), custom_call_target="tpu_custom_call" | custom-call | flops 4294967296 | bytes 6291456 | tf_op jit(solution)/shard_map/local_grid/pallas_call | solution.py:147
  18.4 50.9 %reduce_and_smooth.1 = (f32[16,4,128]{2,1,0:T(4,128)}, f32[16,4,128]{2,1,0:T(4,128)}) custom-call(f32[2,32,128,128]{3,2,1,0:T(8,128)} %get-tuple-element.4.g_ref, f32[2,32,8,128]{3,2,1,0:T(8,128)} %get-tuple-element.5.p_ref, f32[16]{0:T(128)} %age_weight.1, f32[16]{0:T(128)} %dur_weight.1, f32[16]{0:T(128)} %credibility.1), custom_call_target="tpu_custom_call" | custom-call | flops 20971520 | bytes 6291456 | tf_op jit(solution)/shard_map/reduce_and_smooth/pallas_call | solution.py:455
  69.3 1.4 %copy.15 = f32[16,4,128]{2,1,0:T(4,128)} copy(f32[16,4,128]{2,1,0:T(4,128)} %get-tuple-element.8) | data formatting | bytes 65536
  70.6 1.4 %copy.16 = f32[16,4,128]{2,1,0:T(4,128)} copy(f32[16,4,128]{2,1,0:T(4,128)} %get-tuple-element.9) | data formatting | bytes 65536

commit v6 on v4

--- a/solution.py
+++ b/solution.py
@@ -355,6 +355,8 @@
         far = sorted(range(1, n2), key=lambda d: -min(d, n2 - d))
         for d in far:
             send(part.at[i * many + lax.rem(i2 + d, n2)], land2.at[d], s2_send.at[d], s2_recv.at[d], second_axis(d))
+        if len(points) < 3:
+            prior_along_z()
         prior_along_y()
         quarter = 2 * core + side
         grid[quarter] = part[i * many + i2]
@@ -375,11 +377,11 @@
 
     @pl.when(c == 0)
     def _():
-        role(0, 4, y, along_y, 8, z, along_z, {0: nth(0), 1: nth(1), 2: nth(2)})
+        role(0, 4, y, along_y, 8, z, along_z, {0: nth(0), 2: nth(1)})
 
     @pl.when(c == 1)
     def _():
-        role(1, 8, z, along_z, 4, y, along_y, {1: nth(0), 3: nth(1), 5: nth(2)})
+        role(1, 8, z, along_z, 4, y, along_y, {1: nth(0), 4: nth(1), 6: nth(2)})
 
     quarter = 2 * c + side
     t = 2 * z + y // 2

time: 70.7 us -> 71.3 us (level)
  no operation moved by 1% of the time
where the time goes in v6:
time: 71.3 us; the launch traced here: 71 us
  Pallas kernels  67.6 us (95%)
  local copies, waits for them, and re-layouts  2.75 us (4%)
    pallas_call x1, Pallas kernels, smooth(): pl.pallas_call(smooth_kernel, out_shape=(jax.ShapeDtypeStruct((16, 4, 128...  49.9 us
    pallas_call x1, Pallas kernels, grids(): pl.pallas_call(grid_kernel, out_shape=(jax.ShapeDtypeStruct((2, 32, 128,...  17.7 us
    unnamed x2, local copies, waits for them, and re-layouts  2.75 us

profile of v6, /device:TPU:1, one launch (start us, length us, event | category | flops | bytes accessed | tf_op | source)
XLA Modules:
  0.0 71.0 jit_solution(4806228298486718419)
XLA Ops:
  0.6 17.7 %local_grid.1 = (f32[2,32,128,128]{3,2,1,0:T(8,128)}, f32[2,32,8,128]{3,2,1,0:T(8,128)}) custom-call(s32[512]{0:T(512)} %bitcast.15, s32[512,128]{1,0:T(8,128)} %bitcast.8, s32[512,128]{1,0:T(8,128)} %bitcast.9, s32[512,128]{1,0:T(8,128)} %bitcast.10, f32[512,128]{1,0:T(8,128)} %bitcast.11, f32[512,128]{1,0:T(8,128)} %bitcast.12, f32[512,128]{1,0:T(8,128)} %bitcast.13, ...), custom_call_target="tpu_custom_call" | custom-call | flops 4294967296 | bytes 6291456 | tf_op jit(solution)/shard_map/local_grid/pallas_call | solution.py:147
  18.4 49.9 %reduce_and_smooth.1 = (f32[16,4,128]{2,1,0:T(4,128)}, f32[16,4,128]{2,1,0:T(4,128)}) custom-call(f32[2,32,128,128]{3,2,1,0:T(8,128)} %get-tuple-element.4.g_ref, f32[2,32,8,128]{3,2,1,0:T(8,128)} %get-tuple-element.5.p_ref, f32[16]{0:T(128)} %age_weight.1, f32[16]{0:T(128)} %dur_weight.1, f32[16]{0:T(128)} %credibility.1), custom_call_target="tpu_custom_call" | custom-call | flops 20971520 | bytes 6291456 | tf_op jit(solution)/shard_map/reduce_and_smooth/pallas_call | solution.py:457
  68.3 1.4 %copy.15 = f32[16,4,128]{2,1,0:T(4,128)} copy(f32[16,4,128]{2,1,0:T(4,128)} %get-tuple-element.8) | data formatting | bytes 65536
  69.6 1.4 %copy.16 = f32[16,4,128]{2,1,0:T(4,128)} copy(f32[16,4,128]{2,1,0:T(4,128)} %get-tuple-element.9) | data formatting | bytes 65536
